TPU v7x, 256 devices: a whole 4x4x8 slice. The times are simulated.
256 devices in a mesh: ctx: 32 (over z_lo, y, core), exp: 8 (over z_hi, x).
Axes of the slice: x: 4, y: 4, z: 8 (z_hi: 2, z_lo: 4; z = z_hi * 4 + z_lo), core: 2. Of those that a mesh axis runs over, the one named last changes fastest.
Arguments:
- hidden_in: bfloat16 [32768, 2048], P(('ctx', 'exp')), may hold values from -6 to 6
- queries: bfloat16 [32768, 2048], P(('ctx', 'exp')), may hold values from -140 to 140
- keys: bfloat16 [32768, 256], P(('ctx', 'exp')), may hold values from -4.5 to 4.5
- values: bfloat16 [32768, 256], P(('ctx', 'exp')), may hold values from -6 to 6
- doc_ids: int32 [32768], P(('ctx', 'exp')), may hold values from 0 to 255, never falling along the last dimension, each value on 1 to 256 neighbouring positions
- norm_gain: float32 [2048], replicated, may hold values from 0.5 to 1.5
- expert_ids: int32 [32768, 4], P(('ctx', 'exp')), may hold values from 0 to 127, all different within a row; in each aligned block of 128 rows (0 to 127, 128 to 255, ...) at most 6 rows name the same one
- gate_weights: float32 [32768, 4], P(('ctx', 'exp')), may hold values from 0.1 to 1
- w_gate_up: bfloat16 [256, 2048, 384], P(('ctx', 'exp')), may hold values from -0.125 to 0.125
- w_down: bfloat16 [256, 192, 2048], P(('ctx', 'exp')), may hold values from -0.3125 to 0.3125
- grad_out: bfloat16 [32768, 2048], P(('ctx', 'exp')), may hold values from -6 to 6
Outputs:
- output: bfloat16 [32768, 2048], P(('ctx', 'exp'))
- grad_in: bfloat16 [32768, 2048], P(('ctx', 'exp'))
- grad_queries: bfloat16 [32768, 2048], P(('ctx', 'exp'))
- grad_keys: float32 [32768, 256], P(('ctx', 'exp'))
- grad_values: float32 [32768, 256], P(('ctx', 'exp'))
- grad_gate_up: float32 [256, 2048, 384], P(('ctx', 'exp'))
- grad_down: float32 [256, 192, 2048], P(('ctx', 'exp'))
Inputs may be any that keep to these rules, and one draw needn't show every extreme that they name: `doc_ids`: document numbers never fall along the sequence, and one document holds at most 256 positions. `expert_ids`: A row names 4 different experts. Among the rows of one device no expert is named more than 6 times.
All inputs are finite; a program needn't handle non-finite values.
Results may differ from a plain program's by a relative error of at most 0.023.
Values may be sent and summed in bfloat16 or wider, within the bound.
No kernel may reach another device: no remote copies, remote signals or barrier semaphores. Data moves between devices by JAX's collectives and lax.ppermute only.
A program may use at most 192 MiB of HBM per device.

v0:
```python
import jax
import jax.numpy as jnp
from jax import lax
from jax.experimental import pallas as pl
from jax.experimental.layout import Layout, with_layout_constraint
from jax.experimental.pallas import tpu as pltpu
from jax.sharding import Mesh
from jax.sharding import PartitionSpec as P

HEADS = 16
KV_HEADS = 2
HEAD_DIM = 128
GROUP = 8
HALF = 192
RIM = 2

PARTS_GRAD = 1
PARTS_ROWS = 1
PARTS_BACK = 1
PARTS_OUT = 1

VMEM_LIMIT = 60 * 2**20

EPSILON = 1e-06
MASKED = -1e30

ALL = ("zl", "y", "core", "zh", "x")
COLUMN = ("zh", "zl")
PLANE = ("y", "core", "x")

BF16 = jnp.bfloat16
F32 = jnp.float32


def passed_along(block, distance, sources):
    count, line = lax.axis_size(ALL), lax.axis_size("x")
    route = [
        (i, i + distance) for i in range(count) if 0 <= i + distance < count and i % line in sources
    ]
    return lax.ppermute(block, ALL, route)


def blocks_before(block):
    place = lax.axis_index("x")
    near = passed_along(block, 1, (0, 1, 2, 3))
    direct = passed_along(block, 2, (1, 2))
    handed = passed_along(near, 1, (0, 1))
    return [jnp.where((place == 0) | (place == 3), direct, handed), near]


def sums_from_after(far, near):
    place = lax.axis_index("x")
    swap = [(i, i ^ 1) for i in range(lax.axis_size(ALL)) if i % lax.axis_size("x") < 2]
    swapped = lax.ppermute(far, ALL, swap)
    near = jnp.where(place == 0, (near.astype(F32) + swapped.astype(F32)).astype(BF16), near)
    from_near = passed_along(near, -1, (0, 1, 2, 3))
    from_far = passed_along(far, -2, (2, 3))
    from_swapped = passed_along(swapped, -3, (1,))
    return from_near.astype(F32) + jnp.where(place == 2, from_swapped, from_far).astype(F32)


def attend_window(query_rows, window_keys, window_values, visible):
    scale_factor = HEAD_DIM ** (-0.5)
    row_count = query_rows.shape[0]
    query_heads = query_rows.reshape(row_count, KV_HEADS, GROUP, HEAD_DIM)
    key_heads = window_keys.reshape(-1, KV_HEADS, HEAD_DIM)
    value_heads = window_values.reshape(-1, KV_HEADS, HEAD_DIM)
    scores = (
        jnp.einsum("qgmd,kgd->gmqk", query_heads, key_heads, preferred_element_type=F32)
        * scale_factor
    )
    scores = jnp.where(visible[None, None], scores, MASKED)
    row_max = jnp.max(scores, axis=3, keepdims=True)
    exp_terms = jnp.exp(scores - row_max)
    attn_probs = exp_terms / jnp.sum(exp_terms, axis=3, keepdims=True)
    probs_low = attn_probs.astype(BF16)
    mixed_heads = jnp.einsum("gmqk,kgd->qgmd", probs_low, value_heads, preferred_element_type=F32)
    return (
        mixed_heads.reshape(row_count, HEADS * HEAD_DIM).astype(BF16),
        attn_probs,
        probs_low,
    )


def attend_grad(query_rows, window_keys, window_values, attn_out, grad_rows, attn_probs, probs_low):
    scale_factor = HEAD_DIM ** (-0.5)
    row_count = query_rows.shape[0]
    query_heads = query_rows.reshape(row_count, KV_HEADS, GROUP, HEAD_DIM)
    key_heads = window_keys.reshape(-1, KV_HEADS, HEAD_DIM)
    value_heads = window_values.reshape(-1, KV_HEADS, HEAD_DIM)
    grad_heads = grad_rows.reshape(row_count, KV_HEADS, GROUP, HEAD_DIM)
    out_heads = attn_out.reshape(row_count, KV_HEADS, GROUP, HEAD_DIM)
    row_dot = jnp.einsum("qgmd,qgmd->gmq", grad_heads.astype(F32), out_heads.astype(F32))
    grad_probs = jnp.einsum("qgmd,kgd->gmqk", grad_heads, value_heads, preferred_element_type=F32)
    grad_scores = (attn_probs * (grad_probs - row_dot[..., None])).astype(BF16)
    grad_query = (
        jnp.einsum("gmqk,kgd->qgmd", grad_scores, key_heads, preferred_element_type=F32)
        * scale_factor
    )
    grad_key = (
        jnp.einsum("gmqk,qgmd->kgd", grad_scores, query_heads, preferred_element_type=F32)
        * scale_factor
    )
    grad_value = jnp.einsum("gmqk,qgmd->kgd", probs_low, grad_heads, preferred_element_type=F32)
    return (
        grad_query.reshape(row_count, HEADS * HEAD_DIM).astype(BF16),
        grad_key.reshape(-1, KV_HEADS * HEAD_DIM),
        grad_value.reshape(-1, KV_HEADS * HEAD_DIM),
    )


def columns_of(array, parts):
    width = array.shape[1] // parts
    return [array[:, i * width : (i + 1) * width] for i in range(parts)]


def joined(parts):
    return parts[0] if len(parts) == 1 else jnp.concatenate(parts, axis=1)


def across_plane(rows):
    pairs, line = lax.axis_size(PLANE) // lax.axis_size("x"), lax.axis_size("x")
    groups = [[i * line + x for i in range(pairs) for x in places] for places in ((0, 3), (1, 2))]
    count = len(groups[0])
    cut = rows.reshape(count, rows.shape[0] // count, rows.shape[1])
    moved = lax.all_to_all(cut, PLANE, 0, 0, axis_index_groups=groups, tiled=True)
    return moved.reshape(rows.shape)


def cost_of(flops, *arrays):
    return pl.CostEstimate(
        flops=flops,
        bytes_accessed=sum(x.size * x.dtype.itemsize for x in arrays),
        transcendentals=0,
    )


def pick_kernel(chosen_ref, rows_ref, *rest):
    out_ref = rest[-1]
    picked = jnp.dot(chosen_ref[...], rows_ref[...], preferred_element_type=F32)
    if len(rest) == 2:
        picked = picked * rest[0][...]
    out_ref[...] = picked.astype(out_ref.dtype)


def picked_rows(chosen, rows, width, scale=None):
    count, depth = chosen.shape
    tile = 512
    out = jax.ShapeDtypeStruct((count, width), BF16)
    whole = pl.BlockSpec((count, depth), lambda i: (0, 0), pipeline_mode=pl.Buffered(1))
    operands = [chosen, rows]
    specs = [whole, pl.BlockSpec((depth, tile), lambda i: (0, i))]
    if scale is not None:
        operands.append(scale)
        specs.append(pl.BlockSpec((count, 1), lambda i: (0, 0)))
    return pl.pallas_call(
        pick_kernel,
        grid=(width // tile,),
        out_shape=out,
        in_specs=specs,
        out_specs=pl.BlockSpec((count, tile), lambda i: (0, i)),
        compiler_params=pltpu.CompilerParams(vmem_limit_bytes=VMEM_LIMIT),
        cost_estimate=cost_of(2 * count * depth * width, chosen, rows, out),
    )(*operands)


def expert_kernel(rows_ref, weight_ref, grad_act_ref, half_ref, act_ref, gate_ref, up_ref):
    projected = jnp.dot(rows_ref[...], weight_ref[...], preferred_element_type=F32)
    gate_pre = projected[:, : 2 * HALF]
    up_pre = projected[:, 2 * HALF :]
    sigmoid_gate = jax.nn.sigmoid(gate_pre)
    silu = gate_pre * sigmoid_gate
    act_ref[...] = (silu * up_pre).astype(BF16)
    grad_act = grad_act_ref[...]
    grad_gate = (grad_act * up_pre * sigmoid_gate * (1.0 + gate_pre * (1.0 - sigmoid_gate))).astype(
        BF16
    )
    grad_up = (grad_act * silu).astype(BF16)
    gate_ref[...] = grad_gate
    up_ref[...] = grad_up
    half_ref[...] = lax.dot_general(
        jnp.concatenate([grad_gate, grad_up], axis=1),
        weight_ref[...],
        (((1,), (1,)), ((), ())),
        preferred_element_type=F32,
    ).astype(BF16)


def expert_rows(rows, weight_in, grad_act):
    count, width = rows.shape
    hidden = grad_act.shape[1]
    tile = 256
    by_rows = lambda columns: pl.BlockSpec((tile, columns), lambda i: (i, 0))
    outs = [jax.ShapeDtypeStruct((count, c), BF16) for c in (width, hidden, hidden, hidden)]
    return pl.pallas_call(
        expert_kernel,
        grid=(count // tile,),
        out_shape=outs,
        in_specs=[
            by_rows(width),
            pl.BlockSpec(weight_in.shape, lambda i: (0, 0), pipeline_mode=pl.Buffered(1)),
            by_rows(hidden),
        ],
        out_specs=[by_rows(x.shape[1]) for x in outs],
        compiler_params=pltpu.CompilerParams(vmem_limit_bytes=VMEM_LIMIT),
        cost_estimate=cost_of(8 * count * width * hidden, rows, weight_in, grad_act, *outs),
    )(rows, weight_in, grad_act)


def routing_columns(expert_ids, gate_weights):
    high = lax.reduce_precision(gate_weights, 8, 7)
    middle = lax.reduce_precision(gate_weights - high, 8, 7)
    low = gate_weights - high - middle
    columns = jnp.concatenate([expert_ids.astype(F32), high, middle, low], axis=1).astype(BF16)
    return jnp.pad(columns, ((0, 0), (0, 128 - columns.shape[1])))


def route_slots(columns, top):
    planes = lax.axis_size(COLUMN)
    per_plane = lax.axis_size(PLANE) // 2
    tokens = columns.shape[0]
    depth = 3 * tokens * top // (2 * planes * per_plane)
    slots = per_plane * depth
    first = lax.axis_index("zl") * (per_plane * 2) + lax.axis_index("zh") * 2

    def expert_at(place):
        return (first + (place // 2) * 4 + place % 2).astype(F32)

    ids = columns[:, :top].astype(F32)
    experts = expert_at(jnp.arange(per_plane, dtype=jnp.int32))
    named = jnp.any(ids[:, :, None] == experts[None, None, :], axis=1)
    token = jnp.arange(tokens, dtype=jnp.int32)
    before = (token[None, :] < token[:, None]).astype(BF16)
    rank = jnp.dot(before, named.astype(BF16), preferred_element_type=F32)
    rank = jnp.where(named, rank, -1.0).astype(BF16)
    slot = jnp.arange(slots, dtype=jnp.int32)
    place = jnp.arange(per_plane, dtype=jnp.int32)
    spread = (slot[:, None] // depth == place[None, :]).astype(BF16)
    slot_rank = (slot % depth).astype(F32)
    over_tokens = lax.dot_general(
        spread, rank, (((1,), (1,)), ((), ())), preferred_element_type=F32
    )
    chosen = (over_tokens == slot_rank[:, None]).astype(BF16)
    over_slots = lax.dot_general(
        rank, spread, (((1,), (1,)), ((), ())), preferred_element_type=F32
    )
    chosen_back = (over_slots == slot_rank[None, :]).astype(BF16)
    of_slot = jnp.dot(chosen, columns, preferred_element_type=F32)
    gates = (
        of_slot[:, top : 2 * top] + of_slot[:, 2 * top : 3 * top] + of_slot[:, 3 * top : 4 * top]
    )
    mine = of_slot[:, :top] == expert_at(slot // depth)[:, None]
    slot_gate = jnp.sum(jnp.where(mine, gates, 0.0), axis=1, keepdims=True)
    return chosen, chosen_back, slot_gate


def shards(
    hidden_in,
    queries,
    keys,
    values,
    doc_ids,
    norm_gain,
    expert_ids,
    gate_weights,
    w_gate_up,
    w_down,
    grad_out,
):
    row_count = hidden_in.shape[0]
    device_index = lax.axis_index(ALL)
    kv_width = keys.shape[1]

    gathered = []

    def gather_column(part):
        if len(gathered) >= 2:
            part, gathered[-2] = lax.optimization_barrier((part, gathered[-2]))
        rows = lax.all_gather(part, COLUMN, axis=0, tiled=True)
        gathered.append(with_layout_constraint(rows, Layout((0, 1))))

    top = expert_ids.shape[1]
    pieces = columns_of(grad_out, PARTS_GRAD)
    first_width = pieces[0].shape[1]
    pieces[0] = jnp.concatenate([pieces[0], routing_columns(expert_ids, gate_weights)], axis=1)
    for piece in pieces:
        gather_column(piece)

    swap = [(i, i ^ 1) for i in range(lax.axis_size("x"))]
    own_in, own_down = w_gate_up[0], w_down[0]

    doc_columns = jnp.broadcast_to(doc_ids[:, None].astype(BF16), (row_count, 8))
    packed = jnp.concatenate([keys, values, doc_columns], axis=1)
    packed = with_layout_constraint(packed, Layout((1, 0)))
    window_packed = jnp.concatenate(blocks_before(packed) + [packed], axis=0)
    window_packed, own_in, own_down = lax.optimization_barrier((window_packed, own_in, own_down))
    other_down = lax.ppermute(own_down, "x", swap)
    other_in = lax.ppermute(own_in, "x", swap)
    window_keys = window_packed[:, :kv_width]
    window_values = window_packed[:, kv_width : 2 * kv_width]
    window_docs = window_packed[:, 2 * kv_width].astype(jnp.int32)
    query_pos = device_index * row_count + jnp.arange(row_count, dtype=jnp.int32)
    key_pos = (device_index - RIM) * row_count + jnp.arange((RIM + 1) * row_count, dtype=jnp.int32)
    visible = (
        (doc_ids[:, None] == window_docs[None, :])
        & (key_pos[None, :] <= query_pos[:, None])
        & (key_pos[None, :] >= 0)
    )
    attn_out, attn_probs, probs_low = attend_window(queries, window_keys, window_values, visible)
    residual = hidden_in.astype(F32) + attn_out.astype(F32)
    inv_rms = lax.rsqrt(jnp.mean(residual * residual, axis=1, keepdims=True) + EPSILON)
    normed = (residual * inv_rms * norm_gain).astype(BF16)
    normed, other_down = lax.optimization_barrier((normed, other_down))
    for piece in columns_of(normed, PARTS_ROWS):
        if PARTS_GRAD == 1:
            piece, gathered[0] = lax.optimization_barrier((piece, gathered[0]))
        gather_column(piece)
    grad_columns = gathered[:PARTS_GRAD]
    normed_columns = gathered[PARTS_GRAD:]
    chosen, chosen_back, slot_gate = route_slots(grad_columns[0][:, first_width:], top)

    grad_slots = [picked_rows(chosen, part, first_width, slot_gate) for part in grad_columns]
    grad_rows = joined([across_plane(part) for part in grad_slots])
    normed_columns[0], grad_rows, other_in = lax.optimization_barrier(
        (normed_columns[0], grad_rows, other_in)
    )
    weight_in = jnp.concatenate(
        [own_in[:, :HALF], other_in[:, :HALF], own_in[:, HALF:], other_in[:, HALF:]], axis=1
    )
    weight_out = jnp.concatenate([own_down, other_down], axis=0)
    grad_act = lax.dot_general(
        grad_rows, weight_out, (((1,), (1,)), ((), ())), preferred_element_type=F32
    )
    in_rows = joined(
        [across_plane(picked_rows(chosen, part, part.shape[1])) for part in normed_columns]
    )
    back_rows, activated, grad_gate, grad_up = expert_rows(in_rows, weight_in, grad_act)

    chosen_back, _ = lax.optimization_barrier((chosen_back, grad_rows))

    def summed_over_plane(partial):
        return lax.psum_scatter(partial, COLUMN, scatter_dimension=0, tiled=True)

    def added_up(rows):
        return picked_rows(chosen_back, rows, rows.shape[1])

    back_parts = [across_plane(part) for part in columns_of(back_rows, PARTS_BACK)]
    def halves(both, first):
        return both[:, first * HALF : (first + 1) * HALF]

    def times_rows(left, right, out_type):
        return lax.dot_general(
            left, right, (((0,), (0,)), ((), ())), preferred_element_type=F32
        ).astype(out_type)

    own_pre = jnp.concatenate([halves(grad_gate, 0), halves(grad_up, 0)], axis=1)
    other_pre = jnp.concatenate([halves(grad_gate, 1), halves(grad_up, 1)], axis=1)
    sent_in = times_rows(in_rows, other_pre, BF16)
    sent_down = times_rows(halves(activated, 1), grad_rows, BF16)
    kept_in = times_rows(in_rows, own_pre, F32)
    kept_down = times_rows(halves(activated, 0), grad_rows, F32)
    out_rows = [
        jnp.dot(activated, part, preferred_element_type=F32).astype(BF16)
        for part in columns_of(weight_out, PARTS_OUT)
    ]
    back_parts[-1], out_rows[0], sent_in, sent_down, kept_in, kept_down = lax.optimization_barrier(
        (back_parts[-1], out_rows[0], sent_in, sent_down, kept_in, kept_down)
    )
    grad_normed = joined([summed_over_plane(added_up(part)) for part in back_parts]).astype(F32)
    out_parts = [across_plane(part) for part in out_rows]
    sent_in = lax.ppermute(sent_in, "x", swap)
    sent_down = lax.ppermute(sent_down, "x", swap)
    out_sums = [added_up((part.astype(F32) * slot_gate).astype(BF16)) for part in out_parts]
    out_sums[0], sent_in, sent_down = lax.optimization_barrier((out_sums[0], sent_in, sent_down))
    moe_out = joined([summed_over_plane(part) for part in out_sums])

    scaled = norm_gain * grad_normed
    grad_resid = (
        grad_out.astype(F32)
        + inv_rms * scaled
        - residual * inv_rms**3 * jnp.mean(residual * scaled, axis=1, keepdims=True)
    )
    grad_in = grad_resid.astype(BF16)
    grad_queries, key_window_grad, value_window_grad = attend_grad(
        queries, window_keys, window_values, attn_out, grad_in, attn_probs, probs_low
    )
    window_grad = jnp.concatenate([key_window_grad, value_window_grad], axis=1)
    grad_queries, sent_in, sent_down = lax.optimization_barrier((grad_queries, sent_in, sent_down))
    grad_weight_in = kept_in + sent_in.astype(F32)
    grad_weight_out = kept_down + sent_down.astype(F32)
    grad_queries, grad_weight_in, grad_weight_out, moe_out = lax.optimization_barrier(
        (grad_queries, grad_weight_in, grad_weight_out, moe_out)
    )
    output = (residual + moe_out.astype(F32)).astype(BF16)
    far, near = (
        window_grad[i * row_count : (i + 1) * row_count].astype(BF16) for i in range(RIM)
    )
    own_grad = window_grad[RIM * row_count :] + sums_from_after(far, near)
    return (
        output,
        grad_in,
        grad_queries,
        own_grad[:, :kv_width],
        own_grad[:, kv_width:],
        grad_weight_in[None],
        grad_weight_out[None],
    )


def solution(mesh):
    named = Mesh(mesh.devices.reshape(4, 4, 2, 2, 4), ALL)
    rows = P(ALL, None)
    blocks = P(ALL, None, None)
    return jax.shard_map(
        shards,
        mesh=named,
        in_specs=(rows, rows, rows, rows, P(ALL), P(), rows, rows, blocks, blocks, rows),
        out_specs=(rows, rows, rows, rows, rows, blocks, blocks),
        check_vma=False,
    )
```

profile of v0, /device:TPU:1, one launch (start us, length us, event | category | flops | bytes accessed | tf_op | source)
XLA Modules:
  0.0 375.7 jit_solution(14489794971991716359)
XLA Ops:
  13.3 3.9 %collective-permute-start.1 = (bf16[128,520]{0,1:T(8,128)(2,1)S(1)}, bf16[128,520]{0,1:T(8,128)(2,1)S(1)}, u32[]{:S(2)}, u32[]{:S(2)}) collective-permute-start(bf16[128,520]{0,1:T(8,128)(2,1)S(1)} %pad_maximum_fusion.2), channel_id=1, source_target_pairs={{0,1},{1,2},{2,3},{3,4},{4,5},{5,6},{6,7},{7,8},{8,9},{9,10},{10,1... | collective-permute-start | bytes 399368 | tf_op jit(solution)/shard_map/ppermute | solution.py:40
  18.6 10.5 %collective-permute-done.1 = bf16[128,520]{0,1:T(8,128)(2,1)S(1)} collective-permute-done((bf16[128,520]{0,1:T(8,128)(2,1)S(1)}, bf16[128,520]{0,1:T(8,128)(2,1)S(1)}, u32[]{:S(2)}, u32[]{:S(2)}) %collective-permute-start.1) | collective-permute-done | bytes 133152 | tf_op jit(solution)/shard_map/ppermute | solution.py:40
  45.6 15.5 %collective-permute-done.3 = bf16[192,2048]{1,0:T(8,128)(2,1)} collective-permute-done((bf16[192,2048]{1,0:T(8,128)(2,1)}, bf16[192,2048]{1,0:T(8,128)(2,1)}, u32[]{:S(2)}, u32[]{:S(2)}) %collective-permute-start.3) | collective-permute-done | bytes 786464 | tf_op jit(solution)/shard_map/ppermute | solution.py:297
  61.0 10.9 %all-gather.3.cloned.1.call-done.rows_ref = bf16[1024,2176]{1,0:T(8,128)(2,1)} async-done(((bf16[128,2176]{1,0:T(8,128)(2,1)}), bf16[1024,2176]{1,0:T(8,128)(2,1)}) %all-gather.3.cloned.1.call-update) | async-done | bytes 4456464 | tf_op jit(solution)/shard_map/all_gather | solution.py:279
  80.1 7.3 %shard_map.162 = bf16[768,2048]{1,0:T(8,128)(2,1)} custom-call(bf16[768,1024]{1,0:T(8,128)(2,1)} %get-tuple-element.123.chosen_ref, bf16[1024,2176]{1,0:T(8,128)(2,1)} %all-gather.3.cloned.1.call-done.rows_ref, f32[768,1]{1,0:T(8,128)} %broadcast_in_dim.36.rest_0_), custom_call_target="tpu_custom_call" | custom-call | flops 3221225472 | bytes 9175040 | tf_op jit(solution)/shard_map/pallas_call | solution.py:156
  87.4 8.1 %all-to-all-start = ((bf16[16,48,2048]{2,1,0:T(8,128)(2,1)}), bf16[16,48,2048]{2,1,0:T(8,128)(2,1)}, u32[]{:S(2)}, u32[]{:S(2)}) async-start(bf16[16,48,2048]{2,1,0:T(8,128)(2,1)} %bitcast.108), calls=%async_computation | async-start | bytes 6291456 | tf_op jit(solution)/shard_map/all_to_all | solution.py:126
  98.4 34.9 %collective-permute-done.4 = bf16[2048,384]{1,0:T(8,128)(2,1)} collective-permute-done((bf16[2048,384]{1,0:T(8,128)(2,1)}, bf16[2048,384]{1,0:T(8,128)(2,1)}, u32[]{:S(2)}, u32[]{:S(2)}) %collective-permute-start.4) | collective-permute-done | bytes 1572896 | tf_op jit(solution)/shard_map/ppermute | solution.py:298
  133.9 7.2 %shard_map.163 = bf16[768,2048]{1,0:T(8,128)(2,1)} custom-call(bf16[768,1024]{1,0:T(8,128)(2,1)} %get-tuple-element.123.chosen_ref, bf16[1024,2048]{1,0:T(8,128)(2,1)} %all-gather.5.cloned.1.call-done.rows_ref), custom_call_target="tpu_custom_call" | custom-call | flops 3221225472 | bytes 8912896 | tf_op jit(solution)/shard_map/pallas_call | solution.py:156
  141.1 6.1 %all-to-all-start.1 = ((bf16[16,48,2048]{2,1,0:T(8,128)(2,1)}), bf16[16,48,2048]{2,1,0:T(8,128)(2,1)}, u32[]{:S(2)}, u32[]{:S(2)}) async-start(bf16[16,48,2048]{2,1,0:T(8,128)(2,1)} %bitcast.107), calls=%async_computation.1 | async-start | bytes 6291456 | tf_op jit(solution)/shard_map/all_to_all | solution.py:126
  157.6 4.7 %fusion.72.grad_act_ref = f32[768,384]{1,0:T(8,128)} fusion(bf16[768,2048]{1,0:T(8,128)(2,1)} %bitcast.16, bf16[384,2048]{1,0:T(8,128)(2,1)S(1)} %constant_dynamic-update-slice_fusion), kind=kOutput, calls=%fused_computation.143 | convolution fusion | flops 1207959552 | bytes 5898240 | tf_op jit(solution)/shard_map/dot_general | solution.py:331
  162.4 23.3 %all-to-all-done.1 = bf16[16,48,2048]{2,1,0:T(8,128)(2,1)} async-done(((bf16[16,48,2048]{2,1,0:T(8,128)(2,1)}), bf16[16,48,2048]{2,1,0:T(8,128)(2,1)}, u32[]{:S(2)}, u32[]{:S(2)}) %all-to-all-start.1) | async-done | bytes 3145760 | tf_op jit(solution)/shard_map/all_to_all | solution.py:126
  185.6 10.3 %shard_map.164 = (bf16[768,2048]{1,0:T(8,128)(2,1)}, bf16[768,384]{1,0:T(8,128)(2,1)}, bf16[768,384]{1,0:T(8,128)(2,1)}, bf16[768,384]{1,0:T(8,128)(2,1)}) custom-call(bf16[768,2048]{1,0:T(8,128)(2,1)} %bitcast.18.rows_ref, bf16[2048,768]{1,0:T(8,128)(2,1)} %pad_maximum_fusion.weight_ref, f32[768,384]{1,0:T(8,128)} %fusion.72.grad_act_ref), custom_call_target="tpu_custom_call" | custom-call | flops 4831838208 | bytes 12386304 | tf_op jit(solution)/shard_map/pallas_call | solution.py:195
  195.9 5.1 %all-to-all-start.2 = ((bf16[16,48,2048]{2,1,0:T(8,128)(2,1)}), bf16[16,48,2048]{2,1,0:T(8,128)(2,1)}, u32[]{:S(2)}, u32[]{:S(2)}) async-start(bf16[16,48,2048]{2,1,0:T(8,128)(2,1)} %bitcast.106), calls=%async_computation.2 | async-start | bytes 6291456 | tf_op jit(solution)/shard_map/all_to_all | solution.py:126
  208.4 4.0 %fusion.25 = f32[192,2048]{1,0:T(8,128)} fusion(bf16[768,2048]{1,0:T(8,128)(2,1)} %bitcast.16, bf16[768,384]{1,0:T(8,128)(2,1)S(1)} %copy-done.12), kind=kOutput, calls=%fused_computation.57 | convolution fusion | flops 603979776 | bytes 5111808 | tf_op jit(solution)/shard_map/dot_general | solution.py:352
  215.9 5.5 %fusion.19 = f32[2048,384]{1,0:T(8,128)} fusion(bf16[768,2048]{1,0:T(8,128)(2,1)} %bitcast.18.rows_ref, bf16[768,192]{1,0:T(8,128)(2,1)S(1)} %get-tuple-element.110, bf16[768,192]{1,0:T(8,128)(2,1)S(1)} %get-tuple-element.108), kind=kOutput, calls=%fused_computation.48 | convolution fusion | flops 1209139200 | bytes 6881280 | tf_op jit(solution)/shard_map/dot_general | solution.py:352
  221.3 4.9 %convolution_convert_fusion.1 = bf16[2048,384]{1,0:T(8,128)(2,1)} fusion(bf16[768,2048]{1,0:T(8,128)(2,1)} %bitcast.18.rows_ref, bf16[768,192]{1,0:T(8,128)(2,1)S(1)} %get-tuple-element.111, bf16[768,192]{1,0:T(8,128)(2,1)S(1)} %get-tuple-element.109), kind=kOutput, calls=%fused_computation.14 | convolution fusion | flops 1209925632 | bytes 5308416 | tf_op jit(solution)/shard_map/dot_general | solution.py:352
  226.3 13.2 %all-to-all-done.2 = bf16[16,48,2048]{2,1,0:T(8,128)(2,1)} async-done(((bf16[16,48,2048]{2,1,0:T(8,128)(2,1)}), bf16[16,48,2048]{2,1,0:T(8,128)(2,1)}, u32[]{:S(2)}, u32[]{:S(2)}) %all-to-all-start.2) | async-done | bytes 3145760 | tf_op jit(solution)/shard_map/all_to_all | solution.py:126
  239.4 7.2 %shard_map.165 = bf16[1024,2048]{1,0:T(8,128)(2,1)} custom-call(bf16[1024,768]{1,0:T(8,128)(2,1)} %compare_convert_fusion.chosen_ref, bf16[768,2048]{1,0:T(8,128)(2,1)} %bitcast.20.rows_ref), custom_call_target="tpu_custom_call" | custom-call | flops 3221225472 | bytes 8912896 | tf_op jit(solution)/shard_map/pallas_call | solution.py:156
  246.7 5.1 %all-to-all-start.3 = ((bf16[16,48,2048]{2,1,0:T(8,128)(2,1)}), bf16[16,48,2048]{2,1,0:T(8,128)(2,1)}, u32[]{:S(2)}, u32[]{:S(2)}) async-start(bf16[16,48,2048]{2,1,0:T(8,128)(2,1)} %bitcast.105), calls=%async_computation.4 | async-start | bytes 6291456 | tf_op jit(solution)/shard_map/all_to_all | solution.py:126
  253.4 36.8 %all-to-all-done.3 = bf16[16,48,2048]{2,1,0:T(8,128)(2,1)} async-done(((bf16[16,48,2048]{2,1,0:T(8,128)(2,1)}), bf16[16,48,2048]{2,1,0:T(8,128)(2,1)}, u32[]{:S(2)}, u32[]{:S(2)}) %all-to-all-start.3) | async-done | bytes 3145760 | tf_op jit(solution)/shard_map/all_to_all | solution.py:126
  290.2 4.2 %fusion.1.rows_ref = bf16[768,2048]{1,0:T(8,128)(2,1)} fusion(bf16[16,48,2048]{2,1,0:T(8,128)(2,1)} %all-to-all-done.3, f32[768]{0:T(1024)S(1)} %fusion.38), kind=kLoop, calls=%fused_computation.2 | loop fusion | flops 4718592 | bytes 6294528 | tf_op jit(solution)/shard_map/convert_element_type | solution.py:373
  294.4 7.3 %shard_map.166 = bf16[1024,2048]{1,0:T(8,128)(2,1)} custom-call(bf16[1024,768]{1,0:T(8,128)(2,1)} %compare_convert_fusion.chosen_ref, bf16[768,2048]{1,0:T(8,128)(2,1)} %fusion.1.rows_ref), custom_call_target="tpu_custom_call" | custom-call | flops 3221225472 | bytes 8912896 | tf_op jit(solution)/shard_map/pallas_call | solution.py:156
  331.5 11.5 %collective-permute-start.8 = (bf16[128,512]{1,0:T(8,128)(2,1)S(1)}, bf16[128,512]{1,0:T(8,128)(2,1)S(1)}, u32[]{:S(2)}, u32[]{:S(2)}) collective-permute-start(bf16[128,512]{1,0:T(8,128)(2,1)S(1)} %fusion.34), channel_id=1, source_target_pairs={{1,0},{2,1},{3,2},{4,3},{5,4},{6,5},{7,6},{8,7},{9,8},{10,9},{11,1... | collective-permute-start | bytes 393224 | tf_op jit(solution)/shard_map/ppermute | solution.py:40
  350.2 15.9 %reduce-scatter.5.cloned.1.call-done = bf16[128,2048]{1,0:T(8,128)(2,1)} async-done(((bf16[1024,2048]{1,0:T(8,128)(2,1)}), bf16[128,2048]{1,0:T(8,128)(2,1)}) %reduce-scatter.5.cloned.1.call-update) | async-done | bytes 524304 | tf_op jit(solution)/shard_map/reduce_scatter | solution.py:342
  (139 shorter events, 98.0 us)
Async XLA Ops:
  7.2 25.7 %copy-start.19 = (s32[128]{0:T(128)S(1)}, s32[128]{0:T(128)}, u32[]{:S(2)}) copy-start(s32[128]{0:T(128)} %param.15) | copy-start | bytes 1540
  7.2 64.7 %all-gather.3.cloned.1.call-start = ((), (), s32[]{:S(2)}) async-start(), calls=%async_computation.6 | async-start | bytes 5013504 | tf_op jit(solution)/shard_map/all_gather | solution.py:279
  10.7 123.2 %all-gather.5.cloned.1.call-start = ((), (), s32[]{:S(2)}) async-start(), calls=%async_computation.7 | async-start | bytes 4718592 | tf_op jit(solution)/shard_map/all_gather | solution.py:279
  13.3 15.7 %collective-permute-start.1 = (bf16[128,520]{0,1:T(8,128)(2,1)S(1)}, bf16[128,520]{0,1:T(8,128)(2,1)S(1)}, u32[]{:S(2)}, u32[]{:S(2)}) collective-permute-start(bf16[128,520]{0,1:T(8,128)(2,1)S(1)} %pad_maximum_fusion.2), channel_id=1, source_target_pairs={{0,1},{1,2},{2,3},{3,4},{4,5},{5,6},{6,7},{7,8},{8,9},{9,10},{10,1... | collective-permute-start | bytes 399368 | tf_op jit(solution)/shard_map/ppermute | solution.py:40
  17.3 15.4 %collective-permute-start = (bf16[128,520]{0,1:T(8,128)(2,1)S(1)}, bf16[128,520]{0,1:T(8,128)(2,1)S(1)}, u32[]{:S(2)}, u32[]{:S(2)}) collective-permute-start(bf16[128,520]{0,1:T(8,128)(2,1)S(1)} %pad_maximum_fusion.2), channel_id=1, source_target_pairs={{1,3},{2,4},{5,7},{6,8},{9,11},{10,12},{13,15},{14,16},{17,19},{18... | collective-permute-start | bytes 399368 | tf_op jit(solution)/shard_map/ppermute | solution.py:40
  29.1 3.6 collective-permute-start.2
  42.2 18.8 %collective-permute-start.3 = (bf16[192,2048]{1,0:T(8,128)(2,1)}, bf16[192,2048]{1,0:T(8,128)(2,1)}, u32[]{:S(2)}, u32[]{:S(2)}) collective-permute-start(bf16[192,2048]{1,0:T(8,128)(2,1)} %bitcast.119), channel_id=1, source_target_pairs={{0,1},{1,0},{2,3},{3,2},{4,5},{5,4},{6,7},{7,6},{8,9},{9,8},{10,11... | collective-permute-start | bytes 2359304 | tf_op jit(solution)/shard_map/ppermute | solution.py:297
  87.4 46.5 %all-to-all-start = ((bf16[16,48,2048]{2,1,0:T(8,128)(2,1)}), bf16[16,48,2048]{2,1,0:T(8,128)(2,1)}, u32[]{:S(2)}, u32[]{:S(2)}) async-start(bf16[16,48,2048]{2,1,0:T(8,128)(2,1)} %bitcast.108), calls=%async_computation | async-start | bytes 6291456 | tf_op jit(solution)/shard_map/all_to_all | solution.py:126
  95.5 37.8 %collective-permute-start.4 = (bf16[2048,384]{1,0:T(8,128)(2,1)}, bf16[2048,384]{1,0:T(8,128)(2,1)}, u32[]{:S(2)}, u32[]{:S(2)}) collective-permute-start(bf16[2048,384]{1,0:T(8,128)(2,1)} %bitcast.110), channel_id=1, source_target_pairs={{0,1},{1,0},{2,3},{3,2},{4,5},{5,4},{6,7},{7,6},{8,9},{9,8},{10,11... | collective-permute-start | bytes 4718600 | tf_op jit(solution)/shard_map/ppermute | solution.py:298
  141.1 44.5 %all-to-all-start.1 = ((bf16[16,48,2048]{2,1,0:T(8,128)(2,1)}), bf16[16,48,2048]{2,1,0:T(8,128)(2,1)}, u32[]{:S(2)}, u32[]{:S(2)}) async-start(bf16[16,48,2048]{2,1,0:T(8,128)(2,1)} %bitcast.107), calls=%async_computation.1 | async-start | bytes 6291456 | tf_op jit(solution)/shard_map/all_to_all | solution.py:126
  195.9 43.5 %all-to-all-start.2 = ((bf16[16,48,2048]{2,1,0:T(8,128)(2,1)}), bf16[16,48,2048]{2,1,0:T(8,128)(2,1)}, u32[]{:S(2)}, u32[]{:S(2)}) async-start(bf16[16,48,2048]{2,1,0:T(8,128)(2,1)} %bitcast.106), calls=%async_computation.2 | async-start | bytes 6291456 | tf_op jit(solution)/shard_map/all_to_all | solution.py:126
  201.0 105.7 %reduce-scatter.3.cloned.1.call-start = ((), (), s32[]{:S(2)}) async-start(), calls=%async_computation.8 | async-start | bytes 4718592 | tf_op jit(solution)/shard_map/reduce_scatter | solution.py:342
  246.7 43.5 %all-to-all-start.3 = ((bf16[16,48,2048]{2,1,0:T(8,128)(2,1)}), bf16[16,48,2048]{2,1,0:T(8,128)(2,1)}, u32[]{:S(2)}, u32[]{:S(2)}) async-start(bf16[16,48,2048]{2,1,0:T(8,128)(2,1)} %bitcast.105), calls=%async_computation.4 | async-start | bytes 6291456 | tf_op jit(solution)/shard_map/all_to_all | solution.py:126
  251.8 114.4 %reduce-scatter.5.cloned.1.call-start = ((), (), s32[]{:S(2)}) async-start(), calls=%async_computation.9 | async-start | bytes 4718592 | tf_op jit(solution)/shard_map/reduce_scatter | solution.py:342
  251.8 53.0 %collective-permute-start.5 = (bf16[2048,384]{1,0:T(8,128)(2,1)}, bf16[2048,384]{1,0:T(8,128)(2,1)}, u32[]{:S(2)}, u32[]{:S(2)}) collective-permute-start(bf16[2048,384]{1,0:T(8,128)(2,1)} %convolution_convert_fusion.1), channel_id=1, source_target_pairs={{0,1},{1,0},{2,3},{3,2},{4,5},{5,4},{6,7},{7,6},{8,9},{9,8},{10,11... | collective-permute-start | bytes 4718600 | tf_op jit(solution)/shard_map/ppermute | solution.py:371
  251.9 52.9 %collective-permute-start.6 = (bf16[192,2048]{1,0:T(8,128)(2,1)}, bf16[192,2048]{1,0:T(8,128)(2,1)}, u32[]{:S(2)}, u32[]{:S(2)}) collective-permute-start(bf16[192,2048]{1,0:T(8,128)(2,1)} %convolution_convert_fusion.2), channel_id=1, source_target_pairs={{0,1},{1,0},{2,3},{3,2},{4,5},{5,4},{6,7},{7,6},{8,9},{9,8},{10,11... | collective-permute-start | bytes 2359304 | tf_op jit(solution)/shard_map/ppermute | solution.py:372
  321.1 6.8 %copy-start.7 = (f32[2048,384]{1,0:T(8,128)S(1)}, f32[2048,384]{1,0:T(8,128)}, u32[]{:S(2)}) copy-start(f32[2048,384]{1,0:T(8,128)} %fusion.19) | copy-start | bytes 9437188
  322.3 9.1 %collective-permute-start.7 = (bf16[128,512]{1,0:T(8,128)(2,1)S(1)}, bf16[128,512]{1,0:T(8,128)(2,1)S(1)}, u32[]{:S(2)}, u32[]{:S(2)}) collective-permute-start(bf16[128,512]{1,0:T(8,128)(2,1)S(1)} %slice.106), channel_id=1, source_target_pairs={{0,1},{1,0},{4,5},{5,4},{8,9},{9,8},{12,13},{13,12},{16,17},{17,16... | collective-permute-start | bytes 393224 | tf_op jit(solution)/shard_map/ppermute | solution.py:54
  324.4 21.8 %collective-permute-start.10 = (bf16[128,512]{1,0:T(8,128)(2,1)S(1)}, bf16[128,512]{1,0:T(8,128)(2,1)S(1)}, u32[]{:S(2)}, u32[]{:S(2)}) collective-permute-start(bf16[128,512]{1,0:T(8,128)(2,1)S(1)} %slice.106), channel_id=1, source_target_pairs={{2,0},{3,1},{6,4},{7,5},{10,8},{11,9},{14,12},{15,13},{18,16},{19,... | collective-permute-start | bytes 393224 | tf_op jit(solution)/shard_map/ppermute | solution.py:40
  327.8 15.8 %copy-start.2 = (f32[192,2048]{1,0:T(8,128)S(1)}, f32[192,2048]{1,0:T(8,128)}, u32[]{:S(2)}) copy-start(f32[192,2048]{1,0:T(8,128)} %fusion.25) | copy-start | bytes 4718596
  331.4 18.0 %copy-start.6 = (f32[384,256]{1,0:T(8,128)S(1)}, f32[384,256]{1,0:T(8,128)}, u32[]{:S(2)}) copy-start(f32[384,256]{1,0:T(8,128)} %copy.107) | copy-start | bytes 1179652
  331.5 17.9 %collective-permute-start.8 = (bf16[128,512]{1,0:T(8,128)(2,1)S(1)}, bf16[128,512]{1,0:T(8,128)(2,1)S(1)}, u32[]{:S(2)}, u32[]{:S(2)}) collective-permute-start(bf16[128,512]{1,0:T(8,128)(2,1)S(1)} %fusion.34), channel_id=1, source_target_pairs={{1,0},{2,1},{3,2},{4,3},{5,4},{6,5},{7,6},{8,7},{9,8},{10,9},{11,1... | collective-permute-start | bytes 393224 | tf_op jit(solution)/shard_map/ppermute | solution.py:40
  343.0 6.4 %collective-permute-start.9 = (bf16[128,512]{1,0:T(8,128)(2,1)S(1)}, bf16[128,512]{1,0:T(8,128)(2,1)S(1)}, u32[]{:S(2)}, u32[]{:S(2)}) collective-permute-start(bf16[128,512]{1,0:T(8,128)(2,1)S(1)} %collective-permute-done.7), channel_id=1, source_target_pairs={{5,2},{9,6},{13,10},{17,14},{21,18},{25,22},{29,26},{33,30},{37,34... | collective-permute-start | bytes 393224 | tf_op jit(solution)/shard_map/ppermute | solution.py:40
  346.1 22.0 %copy-start.11 = (bf16[2,128,8,128]{3,1,2,0:T(8,128)(2,1)S(1)}, bf16[2,128,8,128]{3,1,2,0:T(8,128)(2,1)}, u32[]{:S(2)}) copy-start(bf16[2,128,8,128]{3,1,2,0:T(8,128)(2,1)} %fusion.9) | copy-start | bytes 1572868
  (15 other events, 54.7 us)
Sparse Core Ops, SparseCore 0:
  10.8 61.0 all-gather.2
  74.3 58.6 all-gather.4
  246.8 52.7 reduce-scatter.2
  304.9 61.1 reduce-scatter.4
where the time goes:
time: 378 us; the launch traced here: 376 us
  waiting for transfers between devices  169 us (45%)
  starting transfers between devices  53.4 us (14%)
  matrix products  42.5 us (11%)
  Pallas kernels  39.3 us (10%)
  other arithmetic  32.9 us (9%)
  local copies, waits for them, and re-layouts  24.3 us (6%)
  between operations  14.3 us (4%)
    all_to_all x4, waiting for transfers between devices, across_plane(): lax.all_to_all(cut, PLANE, 0, 0, axis_index_groups=groups, tiled=True)  73.8 us
    ppermute x1, waiting for transfers between devices, shards(): other_in = lax.ppermute(own_in, 'x', swap)  34.9 us
    pallas_call x4, Pallas kernels, picked_rows(): pl.pallas_call(pick_kernel, grid=(width // tile,), out_shape=out, in_spec...  29 us
    all_to_all x4, starting transfers between devices, across_plane(): lax.all_to_all(cut, PLANE, 0, 0, axis_index_groups=groups, tiled=True)  24.5 us
    ppermute x6, starting transfers between devices, passed_along(): return lax.ppermute(block, ALL, route)  20 us
    dot_general x4, matrix products, times_rows(): lax.dot_general(left, right, (((0,), (0,)), ((), ())), preferred_element_...  18 us
    reduce_scatter x2, waiting for transfers between devices, summed_over_plane(): return lax.psum_scatter(partial, COLUMN, scatter_dimension=0, tiled=True)  15.9 us
    ppermute x1, waiting for transfers between devices, shards(): other_down = lax.ppermute(own_down, 'x', swap)  15.5 us
  transfers between devices with their start and end apart: 19, of which 12 were waited for; matrix products, arithmetic and copies ran while one was open for 25% of the time, Pallas kernels for 4%

commit v1 on v0

--- a/solution.py
+++ b/solution.py
@@ -251,7 +251,8 @@
     )
     mine = of_slot[:, :top] == expert_at(slot // depth)[:, None]
     slot_gate = jnp.sum(jnp.where(mine, gates, 0.0), axis=1, keepdims=True)
-    return chosen, chosen_back, slot_gate
+    gated_back = chosen_back * slot_gate.reshape(1, -1).astype(BF16)
+    return chosen, chosen_back, gated_back, slot_gate
 
 
 def shards(
@@ -317,7 +318,7 @@
         gather_column(piece)
     grad_columns = gathered[:PARTS_GRAD]
     normed_columns = gathered[PARTS_GRAD:]
-    chosen, chosen_back, slot_gate = route_slots(grad_columns[0][:, first_width:], top)
+    chosen, chosen_back, gated_back, slot_gate = route_slots(grad_columns[0][:, first_width:], top)
 
     grad_slots = [picked_rows(chosen, part, first_width, slot_gate) for part in grad_columns]
     grad_rows = joined([across_plane(part) for part in grad_slots])
@@ -336,13 +337,13 @@
     )
     back_rows, activated, grad_gate, grad_up = expert_rows(in_rows, weight_in, grad_act)
 
-    chosen_back, _ = lax.optimization_barrier((chosen_back, grad_rows))
+    chosen_back, gated_back, _ = lax.optimization_barrier((chosen_back, gated_back, grad_rows))
 
     def summed_over_plane(partial):
         return lax.psum_scatter(partial, COLUMN, scatter_dimension=0, tiled=True)
 
-    def added_up(rows):
-        return picked_rows(chosen_back, rows, rows.shape[1])
+    def added_up(weights, rows):
+        return picked_rows(weights, rows, rows.shape[1])
 
     back_parts = [across_plane(part) for part in columns_of(back_rows, PARTS_BACK)]
     def halves(both, first):
@@ -366,15 +367,16 @@
     back_parts[-1], out_rows[0], sent_in, sent_down, kept_in, kept_down = lax.optimization_barrier(
         (back_parts[-1], out_rows[0], sent_in, sent_down, kept_in, kept_down)
     )
-    grad_normed = joined([summed_over_plane(added_up(part)) for part in back_parts]).astype(F32)
+    grad_normed = joined([summed_over_plane(added_up(chosen_back, part)) for part in back_parts])
     out_parts = [across_plane(part) for part in out_rows]
     sent_in = lax.ppermute(sent_in, "x", swap)
+    out_parts[-1], sent_down = lax.optimization_barrier((out_parts[-1], sent_down))
     sent_down = lax.ppermute(sent_down, "x", swap)
-    out_sums = [added_up((part.astype(F32) * slot_gate).astype(BF16)) for part in out_parts]
-    out_sums[0], sent_in, sent_down = lax.optimization_barrier((out_sums[0], sent_in, sent_down))
+    out_sums = [added_up(gated_back, part) for part in out_parts]
+    out_sums[0], sent_in = lax.optimization_barrier((out_sums[0], sent_in))
     moe_out = joined([summed_over_plane(part) for part in out_sums])
 
-    scaled = norm_gain * grad_normed
+    scaled = norm_gain * grad_normed.astype(F32)
     grad_resid = (
         grad_out.astype(F32)
         + inv_rms * scaled

time: 378 us -> 373 us (0.987)
  other arithmetic: 32.9 us -> 28.8 us
    all_gather x2, waiting for transfers between devices: 10.9 us -> 20.2 us  [gather_column(): rows = lax.all_gather(part, COLUMN, axis=0, tiled=True)]
    ppermute x1, waiting for transfers between devices: 15.5 us -> 6.15 us  [shards(): other_down = lax.ppermute(own_down, 'x', swap)]
    convert_element_type x1, other arithmetic: 4.21 us -> 0.01 us  [route_slots(): gated_back = chosen_back * slot_gate.reshape(1, -1).astype(BF16)]
  transfers between devices with their start and end apart: 19 -> 19, of which waited for: 12 -> 12; matrix products, arithmetic and copies ran while one was open for 25% -> 24% of each run, Pallas kernels for 4% -> 4%
where the time goes in v1:
time: 373 us; the launch traced here: 371 us
  waiting for transfers between devices  169 us (45%)
  starting transfers between devices  50.3 us (13%)
  matrix products  44.4 us (12%)
  Pallas kernels  39.4 us (11%)
  other arithmetic  28.8 us (8%)
  local copies, waits for them, and re-layouts  24.7 us (7%)
  between operations  14.3 us (4%)
    all_to_all x4, waiting for transfers between devices, across_plane(): lax.all_to_all(cut, PLANE, 0, 0, axis_index_groups=groups, tiled=True)  75 us
    ppermute x1, waiting for transfers between devices, shards(): other_in = lax.ppermute(own_in, 'x', swap)  34.9 us
    pallas_call x4, Pallas kernels, picked_rows(): pl.pallas_call(pick_kernel, grid=(width // tile,), out_shape=out, in_spec...  29.1 us
    all_to_all x4, starting transfers between devices, across_plane(): lax.all_to_all(cut, PLANE, 0, 0, axis_index_groups=groups, tiled=True)  24.5 us
    all_gather x2, waiting for transfers between devices, gather_column(): rows = lax.all_gather(part, COLUMN, axis=0, tiled=True)  20.2 us
    reduce_scatter x2, waiting for transfers between devices, summed_over_plane(): return lax.psum_scatter(partial, COLUMN, scatter_dimension=0, tiled=True)  18.7 us
    dot_general x4, matrix products, times_rows(): lax.dot_general(left, right, (((0,), (0,)), ((), ())), preferred_element_...  18 us
    ppermute x6, starting transfers between devices, passed_along(): return lax.ppermute(block, ALL, route)  17.2 us
  transfers between devices with their start and end apart: 19, of which 12 were waited for; matrix products, arithmetic and copies ran while one was open for 24% of the time, Pallas kernels for 4%

profile of v1, /device:TPU:1, one launch (start us, length us, event | category | flops | bytes accessed | tf_op | source)
XLA Modules:
  0.0 371.2 jit_solution(368779045828826159)
XLA Ops:
  13.3 3.9 %collective-permute-start.1 = (bf16[128,520]{0,1:T(8,128)(2,1)S(1)}, bf16[128,520]{0,1:T(8,128)(2,1)S(1)}, u32[]{:S(2)}, u32[]{:S(2)}) collective-permute-start(bf16[128,520]{0,1:T(8,128)(2,1)S(1)} %pad_maximum_fusion.2), channel_id=1, source_target_pairs={{0,1},{1,2},{2,3},{3,4},{4,5},{5,6},{6,7},{7,8},{8,9},{9,10},{10,1... | collective-permute-start | bytes 399368 | tf_op jit(solution)/shard_map/ppermute | solution.py:40
  18.6 10.5 %collective-permute-done.1 = bf16[128,520]{0,1:T(8,128)(2,1)S(1)} collective-permute-done((bf16[128,520]{0,1:T(8,128)(2,1)S(1)}, bf16[128,520]{0,1:T(8,128)(2,1)S(1)}, u32[]{:S(2)}, u32[]{:S(2)}) %collective-permute-start.1) | collective-permute-done | bytes 133152 | tf_op jit(solution)/shard_map/ppermute | solution.py:40
  45.5 6.1 %collective-permute-done.3 = bf16[192,2048]{1,0:T(8,128)(2,1)} collective-permute-done((bf16[192,2048]{1,0:T(8,128)(2,1)}, bf16[192,2048]{1,0:T(8,128)(2,1)}, u32[]{:S(2)}, u32[]{:S(2)}) %collective-permute-start.3) | collective-permute-done | bytes 786464 | tf_op jit(solution)/shard_map/ppermute | solution.py:298
  51.7 20.2 %all-gather.3.cloned.1.call-done.rows_ref = bf16[1024,2176]{1,0:T(8,128)(2,1)} async-done(((bf16[128,2176]{1,0:T(8,128)(2,1)}), bf16[1024,2176]{1,0:T(8,128)(2,1)}) %all-gather.3.cloned.1.call-update) | async-done | bytes 4456464 | tf_op jit(solution)/shard_map/all_gather | solution.py:280
  80.1 7.3 %shard_map.162 = bf16[768,2048]{1,0:T(8,128)(2,1)} custom-call(bf16[768,1024]{1,0:T(8,128)(2,1)} %get-tuple-element.127.chosen_ref, bf16[1024,2176]{1,0:T(8,128)(2,1)} %all-gather.3.cloned.1.call-done.rows_ref, f32[768,1]{1,0:T(8,128)} %broadcast_in_dim.36.rest_0_), custom_call_target="tpu_custom_call" | custom-call | flops 3221225472 | bytes 9175040 | tf_op jit(solution)/shard_map/pallas_call | solution.py:156
  87.4 8.1 %all-to-all-start = ((bf16[16,48,2048]{2,1,0:T(8,128)(2,1)}), bf16[16,48,2048]{2,1,0:T(8,128)(2,1)}, u32[]{:S(2)}, u32[]{:S(2)}) async-start(bf16[16,48,2048]{2,1,0:T(8,128)(2,1)} %bitcast.106), calls=%async_computation | async-start | bytes 6291456 | tf_op jit(solution)/shard_map/all_to_all | solution.py:126
  98.4 34.9 %collective-permute-done.4 = bf16[2048,384]{1,0:T(8,128)(2,1)} collective-permute-done((bf16[2048,384]{1,0:T(8,128)(2,1)}, bf16[2048,384]{1,0:T(8,128)(2,1)}, u32[]{:S(2)}, u32[]{:S(2)}) %collective-permute-start.4) | collective-permute-done | bytes 1572896 | tf_op jit(solution)/shard_map/ppermute | solution.py:299
  133.9 7.2 %shard_map.163 = bf16[768,2048]{1,0:T(8,128)(2,1)} custom-call(bf16[768,1024]{1,0:T(8,128)(2,1)} %get-tuple-element.127.chosen_ref, bf16[1024,2048]{1,0:T(8,128)(2,1)} %all-gather.5.cloned.1.call-done.rows_ref), custom_call_target="tpu_custom_call" | custom-call | flops 3221225472 | bytes 8912896 | tf_op jit(solution)/shard_map/pallas_call | solution.py:156
  141.2 6.1 %all-to-all-start.1 = ((bf16[16,48,2048]{2,1,0:T(8,128)(2,1)}), bf16[16,48,2048]{2,1,0:T(8,128)(2,1)}, u32[]{:S(2)}, u32[]{:S(2)}) async-start(bf16[16,48,2048]{2,1,0:T(8,128)(2,1)} %bitcast.105), calls=%async_computation.1 | async-start | bytes 6291456 | tf_op jit(solution)/shard_map/all_to_all | solution.py:126
  157.7 4.7 %fusion.72.grad_act_ref = f32[768,384]{1,0:T(8,128)} fusion(bf16[768,2048]{1,0:T(8,128)(2,1)} %bitcast.16, bf16[384,2048]{1,0:T(8,128)(2,1)S(1)} %constant_dynamic-update-slice_fusion), kind=kOutput, calls=%fused_computation.143 | convolution fusion | flops 1207959552 | bytes 5898240 | tf_op jit(solution)/shard_map/dot_general | solution.py:332
  162.4 23.3 %all-to-all-done.1 = bf16[16,48,2048]{2,1,0:T(8,128)(2,1)} async-done(((bf16[16,48,2048]{2,1,0:T(8,128)(2,1)}), bf16[16,48,2048]{2,1,0:T(8,128)(2,1)}, u32[]{:S(2)}, u32[]{:S(2)}) %all-to-all-start.1) | async-done | bytes 3145760 | tf_op jit(solution)/shard_map/all_to_all | solution.py:126
  185.7 10.3 %shard_map.164 = (bf16[768,2048]{1,0:T(8,128)(2,1)}, bf16[768,384]{1,0:T(8,128)(2,1)}, bf16[768,384]{1,0:T(8,128)(2,1)}, bf16[768,384]{1,0:T(8,128)(2,1)}) custom-call(bf16[768,2048]{1,0:T(8,128)(2,1)} %bitcast.18.rows_ref, bf16[2048,768]{1,0:T(8,128)(2,1)} %pad_maximum_fusion.weight_ref, f32[768,384]{1,0:T(8,128)} %fusion.72.grad_act_ref), custom_call_target="tpu_custom_call" | custom-call | flops 4831838208 | bytes 12386304 | tf_op jit(solution)/shard_map/pallas_call | solution.py:195
  196.0 5.1 %all-to-all-start.2 = ((bf16[16,48,2048]{2,1,0:T(8,128)(2,1)}), bf16[16,48,2048]{2,1,0:T(8,128)(2,1)}, u32[]{:S(2)}, u32[]{:S(2)}) async-start(bf16[16,48,2048]{2,1,0:T(8,128)(2,1)} %bitcast.103), calls=%async_computation.2 | async-start | bytes 6291456 | tf_op jit(solution)/shard_map/all_to_all | solution.py:126
  205.1 3.7 convolution_convert_fusion.2
  208.8 4.0 %fusion.24 = f32[192,2048]{1,0:T(8,128)} fusion(bf16[768,2048]{1,0:T(8,128)(2,1)} %bitcast.16, bf16[768,384]{1,0:T(8,128)(2,1)S(1)} %copy-done.12), kind=kOutput, calls=%fused_computation.56 | convolution fusion | flops 603979776 | bytes 5111808 | tf_op jit(solution)/shard_map/dot_general | solution.py:353
  216.2 5.4 %fusion.18 = f32[2048,384]{1,0:T(8,128)} fusion(bf16[768,2048]{1,0:T(8,128)(2,1)} %bitcast.18.rows_ref, bf16[768,192]{1,0:T(8,128)(2,1)S(1)} %get-tuple-element.114, bf16[768,192]{1,0:T(8,128)(2,1)S(1)} %get-tuple-element.112), kind=kOutput, calls=%fused_computation.47 | convolution fusion | flops 1209139200 | bytes 6881280 | tf_op jit(solution)/shard_map/dot_general | solution.py:353
  221.7 4.9 %convolution_convert_fusion.1 = bf16[2048,384]{1,0:T(8,128)(2,1)} fusion(bf16[768,2048]{1,0:T(8,128)(2,1)} %bitcast.18.rows_ref, bf16[768,192]{1,0:T(8,128)(2,1)S(1)} %get-tuple-element.115, bf16[768,192]{1,0:T(8,128)(2,1)S(1)} %get-tuple-element.113), kind=kOutput, calls=%fused_computation.11 | convolution fusion | flops 1209925632 | bytes 5308416 | tf_op jit(solution)/shard_map/dot_general | solution.py:353
  226.6 12.8 %all-to-all-done.2 = bf16[16,48,2048]{2,1,0:T(8,128)(2,1)} async-done(((bf16[16,48,2048]{2,1,0:T(8,128)(2,1)}), bf16[16,48,2048]{2,1,0:T(8,128)(2,1)}, u32[]{:S(2)}, u32[]{:S(2)}) %all-to-all-start.2) | async-done | bytes 3145760 | tf_op jit(solution)/shard_map/all_to_all | solution.py:126
  239.5 7.3 %shard_map.165 = bf16[1024,2048]{1,0:T(8,128)(2,1)} custom-call(bf16[1024,768]{1,0:T(8,128)(2,1)} %get-tuple-element.47.chosen_ref, bf16[768,2048]{1,0:T(8,128)(2,1)} %bitcast.20.rows_ref), custom_call_target="tpu_custom_call" | custom-call | flops 3221225472 | bytes 8912896 | tf_op jit(solution)/shard_map/pallas_call | solution.py:156
  246.7 5.1 %all-to-all-start.3 = ((bf16[16,48,2048]{2,1,0:T(8,128)(2,1)}), bf16[16,48,2048]{2,1,0:T(8,128)(2,1)}, u32[]{:S(2)}, u32[]{:S(2)}) async-start(bf16[16,48,2048]{2,1,0:T(8,128)(2,1)} %bitcast.104), calls=%async_computation.4 | async-start | bytes 6291456 | tf_op jit(solution)/shard_map/all_to_all | solution.py:126
  252.0 38.2 %all-to-all-done.3 = bf16[16,48,2048]{2,1,0:T(8,128)(2,1)} async-done(((bf16[16,48,2048]{2,1,0:T(8,128)(2,1)}), bf16[16,48,2048]{2,1,0:T(8,128)(2,1)}, u32[]{:S(2)}, u32[]{:S(2)}) %all-to-all-start.3) | async-done | bytes 3145760 | tf_op jit(solution)/shard_map/all_to_all | solution.py:126
  290.2 7.3 %shard_map.166 = bf16[1024,2048]{1,0:T(8,128)(2,1)} custom-call(bf16[1024,768]{1,0:T(8,128)(2,1)} %broadcast_select_fusion.chosen_ref, bf16[768,2048]{1,0:T(8,128)(2,1)} %bitcast.26.rows_ref), custom_call_target="tpu_custom_call" | custom-call | flops 3221225472 | bytes 8912896 | tf_op jit(solution)/shard_map/pallas_call | solution.py:156
  327.6 8.8 %collective-permute-start.8 = (bf16[128,512]{1,0:T(8,128)(2,1)S(1)}, bf16[128,512]{1,0:T(8,128)(2,1)S(1)}, u32[]{:S(2)}, u32[]{:S(2)}) collective-permute-start(bf16[128,512]{1,0:T(8,128)(2,1)S(1)} %fusion.33), channel_id=1, source_target_pairs={{1,0},{2,1},{3,2},{4,3},{5,4},{6,5},{7,6},{8,7},{9,8},{10,9},{11,1... | collective-permute-start | bytes 393224 | tf_op jit(solution)/shard_map/ppermute | solution.py:40
  343.2 18.5 %reduce-scatter.5.cloned.1.call-done = bf16[128,2048]{1,0:T(8,128)(2,1)} async-done(((bf16[1024,2048]{1,0:T(8,128)(2,1)}), bf16[128,2048]{1,0:T(8,128)(2,1)}) %reduce-scatter.5.cloned.1.call-update) | async-done | bytes 524304 | tf_op jit(solution)/shard_map/reduce_scatter | solution.py:343
  (140 shorter events, 93.0 us)
Async XLA Ops:
  7.2 27.9 %copy-start.19 = (s32[128]{0:T(128)S(1)}, s32[128]{0:T(128)}, u32[]{:S(2)}) copy-start(s32[128]{0:T(128)} %param.15) | copy-start | bytes 1540
  7.2 64.7 %all-gather.3.cloned.1.call-start = ((), (), s32[]{:S(2)}) async-start(), calls=%async_computation.6 | async-start | bytes 5013504 | tf_op jit(solution)/shard_map/all_gather | solution.py:280
  10.7 123.3 %all-gather.5.cloned.1.call-start = ((), (), s32[]{:S(2)}) async-start(), calls=%async_computation.7 | async-start | bytes 4718592 | tf_op jit(solution)/shard_map/all_gather | solution.py:280
  13.3 15.7 %collective-permute-start.1 = (bf16[128,520]{0,1:T(8,128)(2,1)S(1)}, bf16[128,520]{0,1:T(8,128)(2,1)S(1)}, u32[]{:S(2)}, u32[]{:S(2)}) collective-permute-start(bf16[128,520]{0,1:T(8,128)(2,1)S(1)} %pad_maximum_fusion.2), channel_id=1, source_target_pairs={{0,1},{1,2},{2,3},{3,4},{4,5},{5,6},{6,7},{7,8},{8,9},{9,10},{10,1... | collective-permute-start | bytes 399368 | tf_op jit(solution)/shard_map/ppermute | solution.py:40
  17.3 15.4 %collective-permute-start = (bf16[128,520]{0,1:T(8,128)(2,1)S(1)}, bf16[128,520]{0,1:T(8,128)(2,1)S(1)}, u32[]{:S(2)}, u32[]{:S(2)}) collective-permute-start(bf16[128,520]{0,1:T(8,128)(2,1)S(1)} %pad_maximum_fusion.2), channel_id=1, source_target_pairs={{1,3},{2,4},{5,7},{6,8},{9,11},{10,12},{13,15},{14,16},{17,19},{18... | collective-permute-start | bytes 399368 | tf_op jit(solution)/shard_map/ppermute | solution.py:40
  29.1 3.6 collective-permute-start.2
  32.8 18.9 %collective-permute-start.3 = (bf16[192,2048]{1,0:T(8,128)(2,1)}, bf16[192,2048]{1,0:T(8,128)(2,1)}, u32[]{:S(2)}, u32[]{:S(2)}) collective-permute-start(bf16[192,2048]{1,0:T(8,128)(2,1)} %bitcast.3), channel_id=1, source_target_pairs={{0,1},{1,0},{2,3},{3,2},{4,5},{5,4},{6,7},{7,6},{8,9},{9,8},{10,11... | collective-permute-start | bytes 2359304 | tf_op jit(solution)/shard_map/ppermute | solution.py:298
  87.4 46.5 %all-to-all-start = ((bf16[16,48,2048]{2,1,0:T(8,128)(2,1)}), bf16[16,48,2048]{2,1,0:T(8,128)(2,1)}, u32[]{:S(2)}, u32[]{:S(2)}) async-start(bf16[16,48,2048]{2,1,0:T(8,128)(2,1)} %bitcast.106), calls=%async_computation | async-start | bytes 6291456 | tf_op jit(solution)/shard_map/all_to_all | solution.py:126
  95.6 37.8 %collective-permute-start.4 = (bf16[2048,384]{1,0:T(8,128)(2,1)}, bf16[2048,384]{1,0:T(8,128)(2,1)}, u32[]{:S(2)}, u32[]{:S(2)}) collective-permute-start(bf16[2048,384]{1,0:T(8,128)(2,1)} %bitcast.108), channel_id=1, source_target_pairs={{0,1},{1,0},{2,3},{3,2},{4,5},{5,4},{6,7},{7,6},{8,9},{9,8},{10,11... | collective-permute-start | bytes 4718600 | tf_op jit(solution)/shard_map/ppermute | solution.py:299
  141.2 44.5 %all-to-all-start.1 = ((bf16[16,48,2048]{2,1,0:T(8,128)(2,1)}), bf16[16,48,2048]{2,1,0:T(8,128)(2,1)}, u32[]{:S(2)}, u32[]{:S(2)}) async-start(bf16[16,48,2048]{2,1,0:T(8,128)(2,1)} %bitcast.105), calls=%async_computation.1 | async-start | bytes 6291456 | tf_op jit(solution)/shard_map/all_to_all | solution.py:126
  196.0 43.5 %all-to-all-start.2 = ((bf16[16,48,2048]{2,1,0:T(8,128)(2,1)}), bf16[16,48,2048]{2,1,0:T(8,128)(2,1)}, u32[]{:S(2)}, u32[]{:S(2)}) async-start(bf16[16,48,2048]{2,1,0:T(8,128)(2,1)} %bitcast.103), calls=%async_computation.2 | async-start | bytes 6291456 | tf_op jit(solution)/shard_map/all_to_all | solution.py:126
  201.1 98.6 %reduce-scatter.3.cloned.1.call-start = ((), (), s32[]{:S(2)}) async-start(), calls=%async_computation.8 | async-start | bytes 4718592 | tf_op jit(solution)/shard_map/reduce_scatter | solution.py:343
  246.7 43.5 %all-to-all-start.3 = ((bf16[16,48,2048]{2,1,0:T(8,128)(2,1)}), bf16[16,48,2048]{2,1,0:T(8,128)(2,1)}, u32[]{:S(2)}, u32[]{:S(2)}) async-start(bf16[16,48,2048]{2,1,0:T(8,128)(2,1)} %bitcast.104), calls=%async_computation.4 | async-start | bytes 6291456 | tf_op jit(solution)/shard_map/all_to_all | solution.py:126
  251.8 109.8 %reduce-scatter.5.cloned.1.call-start = ((), (), s32[]{:S(2)}) async-start(), calls=%async_computation.9 | async-start | bytes 4718592 | tf_op jit(solution)/shard_map/reduce_scatter | solution.py:343
  251.9 45.6 %collective-permute-start.5 = (bf16[2048,384]{1,0:T(8,128)(2,1)}, bf16[2048,384]{1,0:T(8,128)(2,1)}, u32[]{:S(2)}, u32[]{:S(2)}) collective-permute-start(bf16[2048,384]{1,0:T(8,128)(2,1)} %convolution_convert_fusion.1), channel_id=1, source_target_pairs={{0,1},{1,0},{2,3},{3,2},{4,5},{5,4},{6,7},{7,6},{8,9},{9,8},{10,11... | collective-permute-start | bytes 4718600 | tf_op jit(solution)/shard_map/ppermute | solution.py:372
  299.4 24.6 %collective-permute-start.6 = (bf16[192,2048]{1,0:T(8,128)(2,1)}, bf16[192,2048]{1,0:T(8,128)(2,1)}, u32[]{:S(2)}, u32[]{:S(2)}) collective-permute-start(bf16[192,2048]{1,0:T(8,128)(2,1)} %convolution_convert_fusion.2), channel_id=1, source_target_pairs={{0,1},{1,0},{2,3},{3,2},{4,5},{5,4},{6,7},{7,6},{8,9},{9,8},{10,11... | collective-permute-start | bytes 2359304 | tf_op jit(solution)/shard_map/ppermute | solution.py:374
  316.1 7.8 %copy-start.8 = (f32[2048,384]{1,0:T(8,128)S(1)}, f32[2048,384]{1,0:T(8,128)}, u32[]{:S(2)}) copy-start(f32[2048,384]{1,0:T(8,128)} %fusion.18) | copy-start | bytes 9437188
  317.4 22.2 %collective-permute-start.10 = (bf16[128,512]{1,0:T(8,128)(2,1)S(1)}, bf16[128,512]{1,0:T(8,128)(2,1)S(1)}, u32[]{:S(2)}, u32[]{:S(2)}) collective-permute-start(bf16[128,512]{1,0:T(8,128)(2,1)S(1)} %slice.106), channel_id=1, source_target_pairs={{2,0},{3,1},{6,4},{7,5},{10,8},{11,9},{14,12},{15,13},{18,16},{19,... | collective-permute-start | bytes 393224 | tf_op jit(solution)/shard_map/ppermute | solution.py:40
  318.7 8.9 %collective-permute-start.7 = (bf16[128,512]{1,0:T(8,128)(2,1)S(1)}, bf16[128,512]{1,0:T(8,128)(2,1)S(1)}, u32[]{:S(2)}, u32[]{:S(2)}) collective-permute-start(bf16[128,512]{1,0:T(8,128)(2,1)S(1)} %slice.106), channel_id=1, source_target_pairs={{0,1},{1,0},{4,5},{5,4},{8,9},{9,8},{12,13},{13,12},{16,17},{17,16... | collective-permute-start | bytes 393224 | tf_op jit(solution)/shard_map/ppermute | solution.py:54
  324.0 13.1 %copy-start.2 = (f32[192,2048]{1,0:T(8,128)S(1)}, f32[192,2048]{1,0:T(8,128)}, u32[]{:S(2)}) copy-start(f32[192,2048]{1,0:T(8,128)} %fusion.24) | copy-start | bytes 4718596
  327.6 14.8 %copy-start.7 = (f32[384,256]{1,0:T(8,128)S(1)}, f32[384,256]{1,0:T(8,128)}, u32[]{:S(2)}) copy-start(f32[384,256]{1,0:T(8,128)} %copy.107) | copy-start | bytes 1179652
  327.6 14.8 %collective-permute-start.8 = (bf16[128,512]{1,0:T(8,128)(2,1)S(1)}, bf16[128,512]{1,0:T(8,128)(2,1)S(1)}, u32[]{:S(2)}, u32[]{:S(2)}) collective-permute-start(bf16[128,512]{1,0:T(8,128)(2,1)S(1)} %fusion.33), channel_id=1, source_target_pairs={{1,0},{2,1},{3,2},{4,3},{5,4},{6,5},{7,6},{8,7},{9,8},{10,9},{11,1... | collective-permute-start | bytes 393224 | tf_op jit(solution)/shard_map/ppermute | solution.py:40
  336.4 6.0 %collective-permute-start.9 = (bf16[128,512]{1,0:T(8,128)(2,1)S(1)}, bf16[128,512]{1,0:T(8,128)(2,1)S(1)}, u32[]{:S(2)}, u32[]{:S(2)}) collective-permute-start(bf16[128,512]{1,0:T(8,128)(2,1)S(1)} %collective-permute-done.7), channel_id=1, source_target_pairs={{5,2},{9,6},{13,10},{17,14},{21,18},{25,22},{29,26},{33,30},{37,34... | collective-permute-start | bytes 393224 | tf_op jit(solution)/shard_map/ppermute | solution.py:40
  339.6 24.1 %copy-start.11 = (bf16[2,128,8,128]{3,1,2,0:T(8,128)(2,1)S(1)}, bf16[2,128,8,128]{3,1,2,0:T(8,128)(2,1)}, u32[]{:S(2)}) copy-start(bf16[2,128,8,128]{3,1,2,0:T(8,128)(2,1)} %fusion.8) | copy-start | bytes 1572868
  (15 other events, 46.7 us)
Sparse Core Ops, SparseCore 0:
  10.8 61.0 all-gather.2
  74.2 58.6 all-gather.4
  246.9 52.7 reduce-scatter.2
  302.1 59.5 reduce-scatter.4

commit v2 on v1

--- a/solution.py
+++ b/solution.py
@@ -145,20 +145,20 @@
 
 def picked_rows(chosen, rows, width, scale=None):
     count, depth = chosen.shape
-    tile = 512
+    tile = count // 2
     out = jax.ShapeDtypeStruct((count, width), BF16)
-    whole = pl.BlockSpec((count, depth), lambda i: (0, 0), pipeline_mode=pl.Buffered(1))
+    whole = pl.BlockSpec((depth, width), lambda i: (0, 0), pipeline_mode=pl.Buffered(1))
     operands = [chosen, rows]
-    specs = [whole, pl.BlockSpec((depth, tile), lambda i: (0, i))]
+    specs = [pl.BlockSpec((tile, depth), lambda i: (i, 0)), whole]
     if scale is not None:
         operands.append(scale)
-        specs.append(pl.BlockSpec((count, 1), lambda i: (0, 0)))
+        specs.append(pl.BlockSpec((tile, 1), lambda i: (i, 0)))
     return pl.pallas_call(
         pick_kernel,
-        grid=(width // tile,),
+        grid=(count // tile,),
         out_shape=out,
         in_specs=specs,
-        out_specs=pl.BlockSpec((count, tile), lambda i: (0, i)),
+        out_specs=pl.BlockSpec((tile, width), lambda i: (i, 0)),
         compiler_params=pltpu.CompilerParams(vmem_limit_bytes=VMEM_LIMIT),
         cost_estimate=cost_of(2 * count * depth * width, chosen, rows, out),
     )(*operands)
@@ -390,8 +390,8 @@
     grad_queries, sent_in, sent_down = lax.optimization_barrier((grad_queries, sent_in, sent_down))
     grad_weight_in = kept_in + sent_in.astype(F32)
     grad_weight_out = kept_down + sent_down.astype(F32)
-    grad_queries, grad_weight_in, grad_weight_out, moe_out = lax.optimization_barrier(
-        (grad_queries, grad_weight_in, grad_weight_out, moe_out)
+    grad_weight_in, grad_weight_out, moe_out = lax.optimization_barrier(
+        (grad_weight_in, grad_weight_out, moe_out)
     )
     output = (residual + moe_out.astype(F32)).astype(BF16)
     far, near = (

time: 373 us -> 372 us (level)
  waiting for transfers between devices: 169 us -> 164 us
    all_gather x2, waiting for transfers between devices: 20.2 us -> 10.9 us  [gather_column(): rows = lax.all_gather(part, COLUMN, axis=0, tiled=True)]
    ppermute x1, waiting for transfers between devices: 6.15 us -> 15.5 us  [shards(): other_down = lax.ppermute(own_down, 'x', swap)]
    reduce_scatter x2, waiting for transfers between devices: 18.7 us -> 13.9 us  [summed_over_plane(): return lax.psum_scatter(partial, COLUMN, scatter_dimension=0, tiled=True)]
    unnamed x46 -> x44, local copies, waits for them, and re-layouts: 7.49 us -> 9.58 us
  transfers between devices with their start and end apart: 19 -> 19, of which waited for: 12 -> 12; matrix products, arithmetic and copies ran while one was open for 24% -> 25% of each run, Pallas kernels for 4% -> 4%
where the time goes in v2:
time: 372 us; the launch traced here: 370 us
  waiting for transfers between devices  164 us (44%)
  starting transfers between devices  52.3 us (14%)
  matrix products  43.9 us (12%)
  Pallas kernels  39.1 us (11%)
  other arithmetic  30.5 us (8%)
  local copies, waits for them, and re-layouts  26.1 us (7%)
  between operations  14.3 us (4%)
    all_to_all x4, waiting for transfers between devices, across_plane(): lax.all_to_all(cut, PLANE, 0, 0, axis_index_groups=groups, tiled=True)  75.2 us
    ppermute x1, waiting for transfers between devices, shards(): other_in = lax.ppermute(own_in, 'x', swap)  34.9 us
    pallas_call x4, Pallas kernels, picked_rows(): pl.pallas_call(pick_kernel, grid=(count // tile,), out_shape=out, in_spec...  28.7 us
    all_to_all x4, starting transfers between devices, across_plane(): lax.all_to_all(cut, PLANE, 0, 0, axis_index_groups=groups, tiled=True)  24.5 us
    ppermute x6, starting transfers between devices, passed_along(): return lax.ppermute(block, ALL, route)  19.1 us
    dot_general x4, matrix products, times_rows(): lax.dot_general(left, right, (((0,), (0,)), ((), ())), preferred_element_...  18 us
    ppermute x1, waiting for transfers between devices, shards(): other_down = lax.ppermute(own_down, 'x', swap)  15.5 us
    reduce_scatter x2, waiting for transfers between devices, summed_over_plane(): return lax.psum_scatter(partial, COLUMN, scatter_dimension=0, tiled=True)  13.9 us
  transfers between devices with their start and end apart: 19, of which 12 were waited for; matrix products, arithmetic and copies ran while one was open for 25% of the time, Pallas kernels for 4%

profile of v2, /device:TPU:1, one launch (start us, length us, event | category | flops | bytes accessed | tf_op | source)
XLA Modules:
  0.0 370.0 jit_solution(13648242185246756993)
XLA Ops:
  13.3 3.9 %collective-permute-start.1 = (bf16[128,520]{0,1:T(8,128)(2,1)S(1)}, bf16[128,520]{0,1:T(8,128)(2,1)S(1)}, u32[]{:S(2)}, u32[]{:S(2)}) collective-permute-start(bf16[128,520]{0,1:T(8,128)(2,1)S(1)} %pad_maximum_fusion.2), channel_id=1, source_target_pairs={{0,1},{1,2},{2,3},{3,4},{4,5},{5,6},{6,7},{7,8},{8,9},{9,10},{10,1... | collective-permute-start | bytes 399368 | tf_op jit(solution)/shard_map/ppermute | solution.py:40
  18.6 10.5 %collective-permute-done.1 = bf16[128,520]{0,1:T(8,128)(2,1)S(1)} collective-permute-done((bf16[128,520]{0,1:T(8,128)(2,1)S(1)}, bf16[128,520]{0,1:T(8,128)(2,1)S(1)}, u32[]{:S(2)}, u32[]{:S(2)}) %collective-permute-start.1) | collective-permute-done | bytes 133152 | tf_op jit(solution)/shard_map/ppermute | solution.py:40
  45.6 15.5 %collective-permute-done.3 = bf16[192,2048]{1,0:T(8,128)(2,1)} collective-permute-done((bf16[192,2048]{1,0:T(8,128)(2,1)}, bf16[192,2048]{1,0:T(8,128)(2,1)}, u32[]{:S(2)}, u32[]{:S(2)}) %collective-permute-start.3) | collective-permute-done | bytes 786464 | tf_op jit(solution)/shard_map/ppermute | solution.py:298
  61.0 10.9 %all-gather.3.cloned.1.call-done.rows_ref = bf16[1024,2176]{1,0:T(8,128)(2,1)} async-done(((bf16[128,2176]{1,0:T(8,128)(2,1)}), bf16[1024,2176]{1,0:T(8,128)(2,1)}) %all-gather.3.cloned.1.call-update) | async-done | bytes 4456464 | tf_op jit(solution)/shard_map/all_gather | solution.py:280
  80.1 7.3 %shard_map.162 = bf16[768,2048]{1,0:T(8,128)(2,1)} custom-call(bf16[768,1024]{1,0:T(8,128)(2,1)} %get-tuple-element.125.chosen_ref, bf16[1024,2176]{1,0:T(8,128)(2,1)} %all-gather.3.cloned.1.call-done.rows_ref, f32[768,1]{1,0:T(8,128)} %broadcast_in_dim.36.rest_0_), custom_call_target="tpu_custom_call" | custom-call | flops 3221225472 | bytes 9175040 | tf_op jit(solution)/shard_map/pallas_call | solution.py:156
  87.4 8.1 %all-to-all-start = ((bf16[16,48,2048]{2,1,0:T(8,128)(2,1)}), bf16[16,48,2048]{2,1,0:T(8,128)(2,1)}, u32[]{:S(2)}, u32[]{:S(2)}) async-start(bf16[16,48,2048]{2,1,0:T(8,128)(2,1)} %bitcast.106), calls=%async_computation | async-start | bytes 6291456 | tf_op jit(solution)/shard_map/all_to_all | solution.py:126
  98.4 34.9 %collective-permute-done.4 = bf16[2048,384]{1,0:T(8,128)(2,1)} collective-permute-done((bf16[2048,384]{1,0:T(8,128)(2,1)}, bf16[2048,384]{1,0:T(8,128)(2,1)}, u32[]{:S(2)}, u32[]{:S(2)}) %collective-permute-start.4) | collective-permute-done | bytes 1572896 | tf_op jit(solution)/shard_map/ppermute | solution.py:299
  133.9 7.2 %shard_map.163 = bf16[768,2048]{1,0:T(8,128)(2,1)} custom-call(bf16[768,1024]{1,0:T(8,128)(2,1)} %get-tuple-element.125.chosen_ref, bf16[1024,2048]{1,0:T(8,128)(2,1)} %all-gather.5.cloned.1.call-done.rows_ref), custom_call_target="tpu_custom_call" | custom-call | flops 3221225472 | bytes 8912896 | tf_op jit(solution)/shard_map/pallas_call | solution.py:156
  141.1 6.1 %all-to-all-start.1 = ((bf16[16,48,2048]{2,1,0:T(8,128)(2,1)}), bf16[16,48,2048]{2,1,0:T(8,128)(2,1)}, u32[]{:S(2)}, u32[]{:S(2)}) async-start(bf16[16,48,2048]{2,1,0:T(8,128)(2,1)} %bitcast.105), calls=%async_computation.1 | async-start | bytes 6291456 | tf_op jit(solution)/shard_map/all_to_all | solution.py:126
  157.6 4.7 %fusion.72.grad_act_ref = f32[768,384]{1,0:T(8,128)} fusion(bf16[768,2048]{1,0:T(8,128)(2,1)} %bitcast.13, bf16[384,2048]{1,0:T(8,128)(2,1)S(1)} %constant_dynamic-update-slice_fusion), kind=kOutput, calls=%fused_computation.143 | convolution fusion | flops 1207959552 | bytes 5898240 | tf_op jit(solution)/shard_map/dot_general | solution.py:332
  162.3 23.3 %all-to-all-done.1 = bf16[16,48,2048]{2,1,0:T(8,128)(2,1)} async-done(((bf16[16,48,2048]{2,1,0:T(8,128)(2,1)}), bf16[16,48,2048]{2,1,0:T(8,128)(2,1)}, u32[]{:S(2)}, u32[]{:S(2)}) %all-to-all-start.1) | async-done | bytes 3145760 | tf_op jit(solution)/shard_map/all_to_all | solution.py:126
  185.6 10.3 %shard_map.164 = (bf16[768,2048]{1,0:T(8,128)(2,1)}, bf16[768,384]{1,0:T(8,128)(2,1)}, bf16[768,384]{1,0:T(8,128)(2,1)}, bf16[768,384]{1,0:T(8,128)(2,1)}) custom-call(bf16[768,2048]{1,0:T(8,128)(2,1)} %bitcast.15.rows_ref, bf16[2048,768]{1,0:T(8,128)(2,1)} %pad_maximum_fusion.weight_ref, f32[768,384]{1,0:T(8,128)} %fusion.72.grad_act_ref), custom_call_target="tpu_custom_call" | custom-call | flops 4831838208 | bytes 12386304 | tf_op jit(solution)/shard_map/pallas_call | solution.py:195
  195.9 5.1 %all-to-all-start.2 = ((bf16[16,48,2048]{2,1,0:T(8,128)(2,1)}), bf16[16,48,2048]{2,1,0:T(8,128)(2,1)}, u32[]{:S(2)}, u32[]{:S(2)}) async-start(bf16[16,48,2048]{2,1,0:T(8,128)(2,1)} %bitcast.103), calls=%async_computation.2 | async-start | bytes 6291456 | tf_op jit(solution)/shard_map/all_to_all | solution.py:126
  204.8 3.7 convolution_convert_fusion.2
  208.5 4.0 %fusion.24 = f32[192,2048]{1,0:T(8,128)} fusion(bf16[768,2048]{1,0:T(8,128)(2,1)} %bitcast.13, bf16[768,384]{1,0:T(8,128)(2,1)S(1)} %copy-done.11), kind=kOutput, calls=%fused_computation.56 | convolution fusion | flops 603979776 | bytes 5111808 | tf_op jit(solution)/shard_map/dot_general | solution.py:353
  215.9 5.4 %fusion.18 = f32[2048,384]{1,0:T(8,128)} fusion(bf16[768,2048]{1,0:T(8,128)(2,1)} %bitcast.15.rows_ref, bf16[768,192]{1,0:T(8,128)(2,1)S(1)} %get-tuple-element.112, bf16[768,192]{1,0:T(8,128)(2,1)S(1)} %get-tuple-element.110), kind=kOutput, calls=%fused_computation.47 | convolution fusion | flops 1209139200 | bytes 6881280 | tf_op jit(solution)/shard_map/dot_general | solution.py:353
  221.3 4.9 %convolution_convert_fusion.1 = bf16[2048,384]{1,0:T(8,128)(2,1)} fusion(bf16[768,2048]{1,0:T(8,128)(2,1)} %bitcast.15.rows_ref, bf16[768,192]{1,0:T(8,128)(2,1)S(1)} %get-tuple-element.113, bf16[768,192]{1,0:T(8,128)(2,1)S(1)} %get-tuple-element.111), kind=kOutput, calls=%fused_computation.11 | convolution fusion | flops 1209925632 | bytes 5308416 | tf_op jit(solution)/shard_map/dot_general | solution.py:353
  226.3 13.1 %all-to-all-done.2 = bf16[16,48,2048]{2,1,0:T(8,128)(2,1)} async-done(((bf16[16,48,2048]{2,1,0:T(8,128)(2,1)}), bf16[16,48,2048]{2,1,0:T(8,128)(2,1)}, u32[]{:S(2)}, u32[]{:S(2)}) %all-to-all-start.2) | async-done | bytes 3145760 | tf_op jit(solution)/shard_map/all_to_all | solution.py:126
  239.4 7.2 %shard_map.165 = bf16[1024,2048]{1,0:T(8,128)(2,1)} custom-call(bf16[1024,768]{1,0:T(8,128)(2,1)} %get-tuple-element.54.chosen_ref, bf16[768,2048]{1,0:T(8,128)(2,1)} %bitcast.17.rows_ref), custom_call_target="tpu_custom_call" | custom-call | flops 3221225472 | bytes 8912896 | tf_op jit(solution)/shard_map/pallas_call | solution.py:156
  246.6 5.1 %all-to-all-start.3 = ((bf16[16,48,2048]{2,1,0:T(8,128)(2,1)}), bf16[16,48,2048]{2,1,0:T(8,128)(2,1)}, u32[]{:S(2)}, u32[]{:S(2)}) async-start(bf16[16,48,2048]{2,1,0:T(8,128)(2,1)} %bitcast.104), calls=%async_computation.4 | async-start | bytes 6291456 | tf_op jit(solution)/shard_map/all_to_all | solution.py:126
  251.8 38.2 %all-to-all-done.3 = bf16[16,48,2048]{2,1,0:T(8,128)(2,1)} async-done(((bf16[16,48,2048]{2,1,0:T(8,128)(2,1)}), bf16[16,48,2048]{2,1,0:T(8,128)(2,1)}, u32[]{:S(2)}, u32[]{:S(2)}) %all-to-all-start.3) | async-done | bytes 3145760 | tf_op jit(solution)/shard_map/all_to_all | solution.py:126
  290.1 7.1 %shard_map.166 = bf16[1024,2048]{1,0:T(8,128)(2,1)} custom-call(bf16[1024,768]{1,0:T(8,128)(2,1)} %broadcast_select_fusion.chosen_ref, bf16[768,2048]{1,0:T(8,128)(2,1)} %bitcast.26.rows_ref), custom_call_target="tpu_custom_call" | custom-call | flops 3221225472 | bytes 8912896 | tf_op jit(solution)/shard_map/pallas_call | solution.py:156
  329.3 10.6 %collective-permute-start.8 = (bf16[128,512]{1,0:T(8,128)(2,1)}, bf16[128,512]{1,0:T(8,128)(2,1)S(1)}, u32[]{:S(2)}, u32[]{:S(2)}) collective-permute-start(bf16[128,512]{1,0:T(8,128)(2,1)} %fusion.33), channel_id=1, source_target_pairs={{1,0},{2,1},{3,2},{4,3},{5,4},{6,5},{7,6},{8,7},{9,8},{10,9},{11,1... | collective-permute-start | bytes 393224 | tf_op jit(solution)/shard_map/ppermute | solution.py:40
  347.8 13.7 %reduce-scatter.5.cloned.1.call-done = bf16[128,2048]{1,0:T(8,128)(2,1)} async-done(((bf16[1024,2048]{1,0:T(8,128)(2,1)}), bf16[128,2048]{1,0:T(8,128)(2,1)}) %reduce-scatter.5.cloned.1.call-update) | async-done | bytes 524304 | tf_op jit(solution)/shard_map/reduce_scatter | solution.py:343
  (138 shorter events, 94.8 us)
Async XLA Ops:
  7.2 25.7 %copy-start.18 = (s32[128]{0:T(128)S(1)}, s32[128]{0:T(128)}, u32[]{:S(2)}) copy-start(s32[128]{0:T(128)} %param.15) | copy-start | bytes 1540
  7.2 64.7 %all-gather.3.cloned.1.call-start = ((), (), s32[]{:S(2)}) async-start(), calls=%async_computation.6 | async-start | bytes 5013504 | tf_op jit(solution)/shard_map/all_gather | solution.py:280
  10.7 123.2 %all-gather.5.cloned.1.call-start = ((), (), s32[]{:S(2)}) async-start(), calls=%async_computation.7 | async-start | bytes 4718592 | tf_op jit(solution)/shard_map/all_gather | solution.py:280
  13.3 15.7 %collective-permute-start.1 = (bf16[128,520]{0,1:T(8,128)(2,1)S(1)}, bf16[128,520]{0,1:T(8,128)(2,1)S(1)}, u32[]{:S(2)}, u32[]{:S(2)}) collective-permute-start(bf16[128,520]{0,1:T(8,128)(2,1)S(1)} %pad_maximum_fusion.2), channel_id=1, source_target_pairs={{0,1},{1,2},{2,3},{3,4},{4,5},{5,6},{6,7},{7,8},{8,9},{9,10},{10,1... | collective-permute-start | bytes 399368 | tf_op jit(solution)/shard_map/ppermute | solution.py:40
  17.3 15.4 %collective-permute-start = (bf16[128,520]{0,1:T(8,128)(2,1)S(1)}, bf16[128,520]{0,1:T(8,128)(2,1)S(1)}, u32[]{:S(2)}, u32[]{:S(2)}) collective-permute-start(bf16[128,520]{0,1:T(8,128)(2,1)S(1)} %pad_maximum_fusion.2), channel_id=1, source_target_pairs={{1,3},{2,4},{5,7},{6,8},{9,11},{10,12},{13,15},{14,16},{17,19},{18... | collective-permute-start | bytes 399368 | tf_op jit(solution)/shard_map/ppermute | solution.py:40
  29.1 3.6 collective-permute-start.2
  38.3 6.1 %copy-start = (bf16[128,2048]{1,0:T(8,128)(2,1)S(1)}, bf16[128,2048]{1,0:T(8,128)(2,1)}, u32[]{:S(2)}) copy-start(bf16[128,2048]{1,0:T(8,128)(2,1)} %param.11) | copy-start | bytes 1572868
  42.2 18.8 %collective-permute-start.3 = (bf16[192,2048]{1,0:T(8,128)(2,1)}, bf16[192,2048]{1,0:T(8,128)(2,1)}, u32[]{:S(2)}, u32[]{:S(2)}) collective-permute-start(bf16[192,2048]{1,0:T(8,128)(2,1)} %bitcast.117), channel_id=1, source_target_pairs={{0,1},{1,0},{2,3},{3,2},{4,5},{5,4},{6,7},{7,6},{8,9},{9,8},{10,11... | collective-permute-start | bytes 2359304 | tf_op jit(solution)/shard_map/ppermute | solution.py:298
  87.4 46.5 %all-to-all-start = ((bf16[16,48,2048]{2,1,0:T(8,128)(2,1)}), bf16[16,48,2048]{2,1,0:T(8,128)(2,1)}, u32[]{:S(2)}, u32[]{:S(2)}) async-start(bf16[16,48,2048]{2,1,0:T(8,128)(2,1)} %bitcast.106), calls=%async_computation | async-start | bytes 6291456 | tf_op jit(solution)/shard_map/all_to_all | solution.py:126
  95.5 37.8 %collective-permute-start.4 = (bf16[2048,384]{1,0:T(8,128)(2,1)}, bf16[2048,384]{1,0:T(8,128)(2,1)}, u32[]{:S(2)}, u32[]{:S(2)}) collective-permute-start(bf16[2048,384]{1,0:T(8,128)(2,1)} %bitcast.108), channel_id=1, source_target_pairs={{0,1},{1,0},{2,3},{3,2},{4,5},{5,4},{6,7},{7,6},{8,9},{9,8},{10,11... | collective-permute-start | bytes 4718600 | tf_op jit(solution)/shard_map/ppermute | solution.py:299
  141.1 44.5 %all-to-all-start.1 = ((bf16[16,48,2048]{2,1,0:T(8,128)(2,1)}), bf16[16,48,2048]{2,1,0:T(8,128)(2,1)}, u32[]{:S(2)}, u32[]{:S(2)}) async-start(bf16[16,48,2048]{2,1,0:T(8,128)(2,1)} %bitcast.105), calls=%async_computation.1 | async-start | bytes 6291456 | tf_op jit(solution)/shard_map/all_to_all | solution.py:126
  151.8 5.8 %copy-start.15 = (bf16[384,2048]{1,0:T(8,128)(2,1)}, bf16[384,2048]{1,0:T(8,128)(2,1)S(1)}, u32[]{:S(2)}) copy-start(bf16[384,2048]{1,0:T(8,128)(2,1)S(1)} %constant_dynamic-update-slice_fusion) | copy-start | bytes 4718596
  195.9 43.5 %all-to-all-start.2 = ((bf16[16,48,2048]{2,1,0:T(8,128)(2,1)}), bf16[16,48,2048]{2,1,0:T(8,128)(2,1)}, u32[]{:S(2)}, u32[]{:S(2)}) async-start(bf16[16,48,2048]{2,1,0:T(8,128)(2,1)} %bitcast.103), calls=%async_computation.2 | async-start | bytes 6291456 | tf_op jit(solution)/shard_map/all_to_all | solution.py:126
  201.0 98.5 %reduce-scatter.3.cloned.1.call-start = ((), (), s32[]{:S(2)}) async-start(), calls=%async_computation.8 | async-start | bytes 4718592 | tf_op jit(solution)/shard_map/reduce_scatter | solution.py:343
  246.6 43.5 %all-to-all-start.3 = ((bf16[16,48,2048]{2,1,0:T(8,128)(2,1)}), bf16[16,48,2048]{2,1,0:T(8,128)(2,1)}, u32[]{:S(2)}, u32[]{:S(2)}) async-start(bf16[16,48,2048]{2,1,0:T(8,128)(2,1)} %bitcast.104), calls=%async_computation.4 | async-start | bytes 6291456 | tf_op jit(solution)/shard_map/all_to_all | solution.py:126
  251.7 109.8 %reduce-scatter.5.cloned.1.call-start = ((), (), s32[]{:S(2)}) async-start(), calls=%async_computation.9 | async-start | bytes 4718592 | tf_op jit(solution)/shard_map/reduce_scatter | solution.py:343
  251.7 45.5 %collective-permute-start.5 = (bf16[2048,384]{1,0:T(8,128)(2,1)}, bf16[2048,384]{1,0:T(8,128)(2,1)}, u32[]{:S(2)}, u32[]{:S(2)}) collective-permute-start(bf16[2048,384]{1,0:T(8,128)(2,1)} %convolution_convert_fusion.1), channel_id=1, source_target_pairs={{0,1},{1,0},{2,3},{3,2},{4,5},{5,4},{6,7},{7,6},{8,9},{9,8},{10,11... | collective-permute-start | bytes 4718600 | tf_op jit(solution)/shard_map/ppermute | solution.py:372
  299.2 25.8 %collective-permute-start.6 = (bf16[192,2048]{1,0:T(8,128)(2,1)}, bf16[192,2048]{1,0:T(8,128)(2,1)}, u32[]{:S(2)}, u32[]{:S(2)}) collective-permute-start(bf16[192,2048]{1,0:T(8,128)(2,1)} %convolution_convert_fusion.2), channel_id=1, source_target_pairs={{0,1},{1,0},{2,3},{3,2},{4,5},{5,4},{6,7},{7,6},{8,9},{9,8},{10,11... | collective-permute-start | bytes 2359304 | tf_op jit(solution)/shard_map/ppermute | solution.py:374
  318.2 6.8 %copy-start.7 = (f32[2048,384]{1,0:T(8,128)S(1)}, f32[2048,384]{1,0:T(8,128)}, u32[]{:S(2)}) copy-start(f32[2048,384]{1,0:T(8,128)} %fusion.18) | copy-start | bytes 9437188
  318.3 10.3 %collective-permute-start.7 = (bf16[128,512]{1,0:T(8,128)(2,1)S(1)}, bf16[128,512]{1,0:T(8,128)(2,1)S(1)}, u32[]{:S(2)}, u32[]{:S(2)}) collective-permute-start(bf16[128,512]{1,0:T(8,128)(2,1)S(1)} %slice.106), channel_id=1, source_target_pairs={{0,1},{1,0},{4,5},{5,4},{8,9},{9,8},{12,13},{13,12},{16,17},{17,16... | collective-permute-start | bytes 393224 | tf_op jit(solution)/shard_map/ppermute | solution.py:54
  321.7 22.4 %collective-permute-start.10 = (bf16[128,512]{1,0:T(8,128)(2,1)S(1)}, bf16[128,512]{1,0:T(8,128)(2,1)}, u32[]{:S(2)}, u32[]{:S(2)}) collective-permute-start(bf16[128,512]{1,0:T(8,128)(2,1)S(1)} %slice.106), channel_id=1, source_target_pairs={{2,0},{3,1},{6,4},{7,5},{10,8},{11,9},{14,12},{15,13},{18,16},{19,... | collective-permute-start | bytes 393224 | tf_op jit(solution)/shard_map/ppermute | solution.py:40
  325.0 15.6 %copy-start.3 = (f32[192,2048]{1,0:T(8,128)S(1)}, f32[192,2048]{1,0:T(8,128)}, u32[]{:S(2)}) copy-start(f32[192,2048]{1,0:T(8,128)} %fusion.24) | copy-start | bytes 4718596
  329.3 16.8 %collective-permute-start.8 = (bf16[128,512]{1,0:T(8,128)(2,1)}, bf16[128,512]{1,0:T(8,128)(2,1)S(1)}, u32[]{:S(2)}, u32[]{:S(2)}) collective-permute-start(bf16[128,512]{1,0:T(8,128)(2,1)} %fusion.33), channel_id=1, source_target_pairs={{1,0},{2,1},{3,2},{4,3},{5,4},{6,5},{7,6},{8,7},{9,8},{10,9},{11,1... | collective-permute-start | bytes 393224 | tf_op jit(solution)/shard_map/ppermute | solution.py:40
  339.9 6.2 %collective-permute-start.9 = (bf16[128,512]{1,0:T(8,128)(2,1)S(1)}, bf16[128,512]{1,0:T(8,128)(2,1)S(1)}, u32[]{:S(2)}, u32[]{:S(2)}) collective-permute-start(bf16[128,512]{1,0:T(8,128)(2,1)S(1)} %collective-permute-done.7), channel_id=1, source_target_pairs={{5,2},{9,6},{13,10},{17,14},{21,18},{25,22},{29,26},{33,30},{37,34... | collective-permute-start | bytes 393224 | tf_op jit(solution)/shard_map/ppermute | solution.py:40
  (14 other events, 43.8 us)
Sparse Core Ops, SparseCore 0:
  10.8 61.0 all-gather.2
  74.3 58.6 all-gather.4
  246.7 52.7 reduce-scatter.2
  301.8 59.5 reduce-scatter.4
